TPU v7x, 256 devices: a whole 4x4x8 slice. The times are simulated.
256 devices in a mesh: dp: 2 (over z_lo), wide: 32 (over x, y, core), mlp: 4 (over z_hi).
Axes of the slice: x: 4, y: 4, z: 8 (z_hi: 4, z_lo: 2; z = z_hi * 2 + z_lo), core: 2. Of those that a mesh axis runs over, the one named last changes fastest.
Arguments:
- inputs: bfloat16 [8, 96, 180, 768], P('dp', 'wide', 'mlp'), may hold values from -6 to 6
- validity: int32 [8, 96, 180], P('dp', 'wide', 'mlp'), may hold values from 0 to 1, as said below
- gain_first: float32 [768], replicated, may hold values from 0.5 to 1.5
- shift_first: float32 [768], replicated, may hold values from -3 to 3
- spectral_in: bfloat16 [2, 8, 96, 96], P(None, 'mlp'), may hold values from -0.4375 to 0.4375
- spectral_in_bias: float32 [2, 8, 96], P(None, 'mlp'), may hold values from -3 to 3
- spectral_out: bfloat16 [2, 8, 96, 96], P(None, 'mlp'), may hold values from -0.15625 to 0.15625
- spectral_out_bias: float32 [2, 8, 96], P(None, 'mlp'), may hold values from -0.6 to 0.6
- gain_second: float32 [768], replicated, may hold values from 0.5 to 1.5
- shift_second: float32 [768], replicated, may hold values from -3 to 3
- weight_in: bfloat16 [768, 3072], P(None, 'mlp'), may hold values from -0.21875 to 0.21875
- bias_in: float32 [3072], P('mlp'), may hold values from -3 to 3
- weight_out: bfloat16 [3072, 768], P('mlp'), may hold values from -0.21875 to 0.21875
- bias_out: float32 [768], replicated, may hold values from -3 to 3
- cotangent: bfloat16 [8, 96, 180, 768], P('dp', 'wide', 'mlp'), may hold values from -6 to 6
Outputs:
- output: bfloat16 [8, 96, 180, 768], P('dp', 'wide', 'mlp')
- grad_inputs: float32 [8, 96, 180, 768], P('dp', 'wide', 'mlp')
- grad_gain_first: float32 [768], P('mlp')
- grad_shift_first: float32 [768], P('mlp')
- grad_spectral_in: float32 [2, 8, 96, 96], replicated
- grad_spectral_in_bias: float32 [2, 8, 96], replicated
- grad_spectral_out: float32 [2, 8, 96, 96], replicated
- grad_spectral_out_bias: float32 [2, 8, 96], replicated
- grad_gain_second: float32 [768], P('mlp')
- grad_shift_second: float32 [768], P('mlp')
- grad_weight_in: float32 [768, 3072], P(None, 'mlp')
- grad_bias_in: float32 [3072], P('mlp')
- grad_weight_out: float32 [3072, 768], P('mlp')
- grad_bias_out: float32 [768], P('mlp')
Inputs may be any that keep to these rules, and one draw needn't show every extreme that they name: `validity`: 1 marks a present patch; the last 6 latitude rows of every snapshot are 0.
All inputs are finite; a program needn't handle non-finite values.
Results may differ from a plain program's by a relative error of at most 0.018.
The roundings to bfloat16 on the way count: a program that leaves them out, or rounds other values in their place, can miss the bound.
Values may be sent and summed in bfloat16 or wider, within the bound.
No kernel may reach another device: no remote copies, remote signals or barrier semaphores. Data moves between devices by JAX's collectives and lax.ppermute only.
A program may use at most 192 MiB of HBM per device.

v0:
```python
import math

import jax
import jax.numpy as jnp
from jax import lax
from jax.sharding import PartitionSpec as P

H = 96
KWP = 96


EPSILON = 1e-05
SHRINK = 0.01


def longitude_tables(length, columns):
    index = jnp.arange(length, dtype=jnp.int32)
    order = jnp.arange(columns, dtype=jnp.int32)
    phase_angle = (index[:, None] * order[None, :] % length).astype(jnp.float32) * (
        2.0 * math.pi / length
    )
    live_scale = jnp.where(order < length // 2 + 1, 1.0 / math.sqrt(length), 0.0).astype(
        jnp.float32
    )
    weight = (
        jnp.where((order == 0) | (2 * order == length), 1.0, 2.0).astype(jnp.float32) * live_scale
    )
    forward = jnp.stack(
        [jnp.cos(phase_angle) * live_scale[None, :], -jnp.sin(phase_angle) * live_scale[None, :]],
        axis=1,
    )
    inverse = jnp.stack(
        [jnp.cos(phase_angle).T * weight[:, None], -jnp.sin(phase_angle).T * weight[:, None]],
        axis=0,
    )
    return (forward, inverse)


def latitude_tables(length):
    index = jnp.arange(length, dtype=jnp.int32)
    phase_angle = (index[:, None] * index[None, :] % length).astype(jnp.float32) * (
        2.0 * math.pi / length
    )
    cosine = jnp.cos(phase_angle) / math.sqrt(length)
    sine_part = jnp.sin(phase_angle) / math.sqrt(length)
    forward = jnp.stack(
        [jnp.stack([cosine, sine_part], axis=1), jnp.stack([-sine_part, cosine], axis=1)], axis=0
    )
    inverse = jnp.stack(
        [jnp.stack([cosine, -sine_part], axis=1), jnp.stack([sine_part, cosine], axis=1)], axis=0
    )
    return (forward, inverse)


def real_form(weights):
    real_part = weights[0]
    imag_part = weights[1]
    upper_rows = jnp.stack([real_part, imag_part], axis=2)
    bottom = jnp.stack([-imag_part, real_part], axis=2)
    return jnp.stack([upper_rows, bottom], axis=1)


def complex_form(gradients):
    real_part = gradients[:, 0, :, 0, :] + gradients[:, 1, :, 1, :]
    imag_part = gradients[:, 0, :, 1, :] - gradients[:, 1, :, 0, :]
    return jnp.stack([real_part, imag_part], axis=0)


def shrink(value):
    return value - SHRINK * value * lax.rsqrt(value * value + SHRINK * SHRINK)


def shrink_slope(value):
    inverse_root = lax.rsqrt(value * value + SHRINK * SHRINK)
    return 1.0 - SHRINK * SHRINK * SHRINK * inverse_root * inverse_root * inverse_root


def gelu_exact(value):
    return jax.nn.gelu(value, approximate=False)


def gelu_back(value, grad):
    return jax.vjp(gelu_exact, value)[1](grad)[0]


def inner_rows(left, right):
    return lax.dot_general(
        left, right, (((0,), (0,)), ((), ())), preferred_element_type=jnp.float32
    )


def outer_cols(left, right):
    return lax.dot_general(
        left, right, (((1,), (1,)), ((), ())), preferred_element_type=jnp.float32
    )


def shards(
    inputs,
    validity,
    gain_first,
    shift_first,
    spectral_in,
    spectral_in_bias,
    spectral_out,
    spectral_out_bias,
    gain_second,
    shift_second,
    weight_in,
    bias_in,
    weight_out,
    bias_out,
    cotangent,
):
    snapshots, lat_rows, lon_here, full_width = inputs.shape
    lon_all = lon_here * lax.axis_size("mlp")
    lon_start = lax.axis_index("mlp") * lon_here
    token_count = snapshots * lat_rows * lon_all
    blocks_here = spectral_in.shape[1]
    block_size = spectral_in.shape[2]
    local_width = blocks_here * block_size
    lon_fwd, lon_inv = longitude_tables(lon_all, KWP)
    lon_fwd = lon_fwd.astype(jnp.bfloat16)
    lon_inv = lon_inv.astype(jnp.bfloat16)
    own_fwd = lax.dynamic_slice_in_dim(lon_fwd, lon_start, lon_here, 0)
    own_inv = lax.dynamic_slice_in_dim(lon_inv, lon_start, lon_here, 2)
    lat_fwd, lat_inv = latitude_tables(H)
    lat_fwd = lat_fwd.astype(jnp.bfloat16)
    lat_inv = lat_inv.astype(jnp.bfloat16)
    real_in = real_form(spectral_in)
    real_out = real_form(spectral_out)
    in_shift = spectral_in_bias[None, None, :, None, :, :]
    out_shift = spectral_out_bias[None, None, :, None, :, :]
    resid = inputs.astype(jnp.float32)
    present = validity.astype(jnp.float32)[..., None]
    centred_first = resid - jnp.mean(resid, axis=3, keepdims=True)
    scale_first = lax.rsqrt(
        jnp.mean(centred_first * centred_first, axis=3, keepdims=True) + EPSILON
    )
    normed_first = centred_first * scale_first
    masked = (normed_first * gain_first + shift_first) * present
    masked_low = masked.astype(jnp.bfloat16)
    partial_spec = jnp.einsum(
        "shwc,wpk->shpkc", masked_low, own_fwd, preferred_element_type=jnp.float32
    )
    spectrum = lax.psum_scatter(partial_spec, "mlp", scatter_dimension=4, tiled=True).astype(
        jnp.bfloat16
    )
    columns = lax.all_to_all(spectrum, "wide", split_axis=3, concat_axis=1, tiled=True)
    number = columns.shape[0]
    freq_cols = columns.shape[3]
    grid_low = jnp.einsum(
        "pjqh,shqkc->sjpkc", lat_fwd, columns, preferred_element_type=jnp.float32
    ).astype(jnp.bfloat16)
    grid_low = grid_low.reshape(number, H, 2, freq_cols, blocks_here, block_size)
    first_layer = (
        jnp.einsum("sjqkbe,bqepf->sjpkbf", grid_low, real_in, preferred_element_type=jnp.float32)
        + in_shift
    )
    active = gelu_exact(first_layer).astype(jnp.bfloat16)
    second = (
        jnp.einsum("sjqkbe,bqepf->sjpkbf", active, real_out, preferred_element_type=jnp.float32)
        + out_shift
    )
    shrunk = shrink(second).astype(jnp.bfloat16).reshape(number, H, 2, freq_cols, local_width)
    back_low = jnp.einsum(
        "pjqh,shqkc->sjpkc", lat_inv, shrunk, preferred_element_type=jnp.float32
    ).astype(jnp.bfloat16)
    back_low, grid_low, active, first_layer, second = (
        back_low,
        grid_low,
        active,
        first_layer,
        second,
    )
    returned = lax.all_to_all(back_low, "wide", split_axis=1, concat_axis=3, tiled=True)
    whole_spec = lax.all_gather(returned, "mlp", axis=4, tiled=True)
    filtered = jnp.einsum(
        "shpkc,pkw->shwc", whole_spec, own_inv, preferred_element_type=jnp.float32
    )
    stream = resid + filtered + masked
    stream_low = stream.astype(jnp.bfloat16).astype(jnp.float32)
    centred = stream_low - jnp.mean(stream_low, axis=3, keepdims=True)
    scale_second = lax.rsqrt(jnp.mean(centred * centred, axis=3, keepdims=True) + EPSILON)
    normed_second = centred * scale_second
    mixed_low = (normed_second * gain_second + shift_second).astype(jnp.bfloat16)
    grad_output = cotangent.astype(jnp.float32)
    grad_branch = grad_output * present
    rows_all, grad_all = (
        lax.all_gather(mixed_low, "mlp", axis=2, tiled=True),
        lax.all_gather(grad_branch.astype(jnp.bfloat16), "mlp", axis=2, tiled=True),
    )
    mixed_rows = rows_all.reshape(token_count, full_width)
    pre_act = jnp.dot(mixed_rows, weight_in, preferred_element_type=jnp.float32) + bias_in
    hidden = gelu_exact(pre_act).astype(jnp.bfloat16)
    partial_rows = jnp.dot(hidden, weight_out, preferred_element_type=jnp.float32).reshape(
        snapshots, lat_rows, lon_all, full_width
    )
    branch = (
        lax.psum_scatter(
            partial_rows.astype(jnp.bfloat16), "mlp", scatter_dimension=2, tiled=True
        ).astype(jnp.float32)
        + bias_out
    )
    output = (stream + present * branch).astype(jnp.bfloat16)
    grad_bias_out = jnp.sum(grad_branch, axis=(0, 1, 2))
    grad_rows = grad_all.reshape(token_count, full_width)
    grad_weight_out = inner_rows(hidden, grad_rows)
    grad_pre = gelu_back(pre_act, outer_cols(grad_rows, weight_out))
    grad_bias_in = jnp.sum(grad_pre, axis=0)
    grad_pre_low = grad_pre.astype(jnp.bfloat16)
    grad_weight_in = inner_rows(mixed_rows, grad_pre_low)
    grad_mixed = outer_cols(grad_pre_low, weight_in).reshape(
        snapshots, lat_rows, lon_all, full_width
    )
    grad_norm = lax.psum_scatter(
        grad_mixed.astype(jnp.bfloat16), "mlp", scatter_dimension=2, tiled=True
    ).astype(jnp.float32)
    grad_gain_second = jnp.sum(grad_norm * normed_second, axis=(0, 1, 2))
    grad_shift_second = jnp.sum(grad_norm, axis=(0, 1, 2))
    scaled = grad_norm * gain_second
    grad_stream = grad_output + scale_second * (
        scaled
        - jnp.mean(scaled, axis=3, keepdims=True)
        - normed_second * jnp.mean(scaled * normed_second, axis=3, keepdims=True)
    )
    grad_stream_low = grad_stream.astype(jnp.bfloat16)
    partial_back = jnp.einsum(
        "shwc,pkw->shpkc", grad_stream_low, own_inv, preferred_element_type=jnp.float32
    )
    grad_back = lax.psum_scatter(partial_back, "mlp", scatter_dimension=4, tiled=True).astype(
        jnp.bfloat16
    )
    grad_columns = lax.all_to_all(grad_back, "wide", split_axis=3, concat_axis=1, tiled=True)
    freq_cols = grad_columns.shape[3]
    grad_shrunk = jnp.einsum(
        "pjqh,sjpkc->shqkc", lat_inv, grad_columns, preferred_element_type=jnp.float32
    )
    grad_second = grad_shrunk.reshape(
        snapshots, H, 2, freq_cols, blocks_here, block_size
    ) * shrink_slope(second)
    grad_out_bias = jnp.sum(grad_second, axis=(0, 1, 3))
    grad_second_low = grad_second.astype(jnp.bfloat16)
    grad_spectral_out = complex_form(
        jnp.einsum(
            "sjqkbe,sjpkbf->bqepf", active, grad_second_low, preferred_element_type=jnp.float32
        )
    )
    grad_first = gelu_back(
        first_layer,
        jnp.einsum(
            "sjpkbf,bqepf->sjqkbe", grad_second_low, real_out, preferred_element_type=jnp.float32
        ),
    )
    grad_in_bias = jnp.sum(grad_first, axis=(0, 1, 3))
    grad_first_low = grad_first.astype(jnp.bfloat16)
    grad_spectral_in = complex_form(
        jnp.einsum(
            "sjqkbe,sjpkbf->bqepf", grid_low, grad_first_low, preferred_element_type=jnp.float32
        )
    )
    grad_grid = jnp.einsum(
        "sjpkbf,bqepf->sjqkbe", grad_first_low, real_in, preferred_element_type=jnp.float32
    ).astype(jnp.bfloat16)
    grad_grid = grad_grid.reshape(snapshots, H, 2, freq_cols, local_width)
    grad_spectrum = jnp.einsum(
        "pjqh,sjpkc->shqkc", lat_fwd, grad_grid, preferred_element_type=jnp.float32
    ).astype(jnp.bfloat16)
    grad_row_spectrum = lax.all_to_all(
        grad_spectrum, "wide", split_axis=1, concat_axis=3, tiled=True
    )
    whole_grad = lax.all_gather(grad_row_spectrum, "mlp", axis=4, tiled=True)
    grad_from_spec = jnp.einsum(
        "shpkc,wpk->shwc", whole_grad, own_fwd, preferred_element_type=jnp.float32
    )
    grad_normed = (grad_from_spec + grad_stream) * present
    grad_gain_first = jnp.sum(grad_normed * normed_first, axis=(0, 1, 2))
    grad_shift_first = jnp.sum(grad_normed, axis=(0, 1, 2))
    scaled_first = grad_normed * gain_first
    grad_inputs = grad_stream + scale_first * (
        scaled_first
        - jnp.mean(scaled_first, axis=3, keepdims=True)
        - normed_first * jnp.mean(scaled_first * normed_first, axis=3, keepdims=True)
    )
    small = (
        lax.psum_scatter(grad_gain_first, "mlp", scatter_dimension=0, tiled=True),
        lax.psum_scatter(grad_shift_first, "mlp", scatter_dimension=0, tiled=True),
        lax.psum_scatter(grad_gain_second, "mlp", scatter_dimension=0, tiled=True),
        lax.psum_scatter(grad_shift_second, "mlp", scatter_dimension=0, tiled=True),
        lax.psum_scatter(grad_bias_out, "mlp", scatter_dimension=0, tiled=True),
    )
    summed = lax.psum(
        (
            grad_weight_in,
            grad_bias_in,
            grad_weight_out,
            small[4],
            small[0],
            small[1],
            small[2],
            small[3],
            grad_spectral_in,
            grad_in_bias,
            grad_spectral_out,
            grad_out_bias,
        ),
        ("dp", "wide"),
    )
    filters = (
        lax.all_gather(summed[8], "mlp", axis=1, tiled=True),
        lax.all_gather(summed[9], "mlp", axis=1, tiled=True),
        lax.all_gather(summed[10], "mlp", axis=1, tiled=True),
        lax.all_gather(summed[11], "mlp", axis=1, tiled=True),
    )
    return (
        output,
        grad_inputs,
        summed[4],
        summed[5],
        filters[0],
        filters[1],
        filters[2],
        filters[3],
        summed[6],
        summed[7],
        summed[0],
        summed[1],
        summed[2],
        summed[3],
    )


def solution(mesh):
    placed = (
        P("dp", "wide", "mlp", None),
        P("dp", "wide", "mlp"),
        P(),
        P(),
        P(None, "mlp", None, None),
        P(None, "mlp", None),
        P(None, "mlp", None, None),
        P(None, "mlp", None),
        P(),
        P(),
        P(None, "mlp"),
        P("mlp"),
        P("mlp", None),
        P(),
        P("dp", "wide", "mlp", None),
    )
    return jax.shard_map(
        shards,
        mesh=mesh,
        in_specs=placed,
        out_specs=(
            P("dp", "wide", "mlp", None),
            P("dp", "wide", "mlp", None),
            P("mlp"),
            P("mlp"),
            P(),
            P(),
            P(),
            P(),
            P("mlp"),
            P("mlp"),
            P(None, "mlp"),
            P("mlp"),
            P("mlp", None),
            P("mlp"),
        ),
        check_vma=False,
    )
```

profile of v0, /device:TPU:1, one launch (start us, length us, event | category | flops | bytes accessed | tf_op | source)
XLA Modules:
  0.0 2047.3 jit_solution(16255558476115232114)
XLA Ops:
  16.2 12.6 copy.290
  28.8 14.7 reshape.513
  44.4 133.5 %reduce-scatter.7.cloned.1.call-done = f32[192,2304]{1,0:T(8,128)} async-done(((f32[768,2304]{1,0:T(8,128)}), f32[192,2304]{1,0:T(8,128)}) %reduce-scatter.7.cloned.1.call-update) | async-done | bytes 1769488
  190.0 8.4 all-to-all-start
  199.1 17.7 all-to-all-done
  221.2 6.1 fusion.68
  238.9 22.9 %all_to_all.72 = bf16[4,96,2,3,192]{4,2,3,0,1:T(2,128)(2,1)S(1)} all-to-all(bf16[4,96,2,3,192]{4,2,3,0,1:T(2,128)(2,1)} %copy.172), channel_id=1, replica_groups=mesh['dp'=2,'wide'=32,'mlp'=4] {'wide'}, dimensions={1} | all-to-all | bytes 1769472 | tf_op jit(solution)/shard_map/all_to_all | solution.py:176
  271.8 75.1 %all-gather.5.cloned.1.call-done = bf16[4,3,2,96,768]{3,0,2,1,4:T(4,128)(2,1)} async-done(((bf16[4,3,2,96,192]{3,0,2,1,4:T(4,128)(2,1)}), bf16[4,3,2,96,768]{3,0,2,1,4:T(4,128)(2,1)}) %all-gather.5.cloned.1.call-update) | async-done | bytes 3538960 | tf_op jit(solution)/shard_map/all_gather | solution.py:177
  354.3 69.9 %all-gather.9.cloned.1.call-done = bf16[4,3,180,768]{3,0,1,2:T(4,128)(2,1)} async-done(((bf16[4,3,45,768]{3,0,1,2:T(4,128)(2,1)}), bf16[4,3,180,768]{3,0,1,2:T(4,128)(2,1)}) %all-gather.9.cloned.1.call-update) | async-done | bytes 3317776 | tf_op jit(solution)/shard_map/all_gather | solution.py:191
  428.2 5.8 reshape.474
  434.0 62.7 %all-gather.7.cloned.1.call-done = bf16[4,3,180,768]{3,0,1,2:T(4,128)(2,1)} async-done(((bf16[4,3,45,768]{3,0,1,2:T(4,128)(2,1)}), bf16[4,3,180,768]{3,0,1,2:T(4,128)(2,1)}) %all-gather.7.cloned.1.call-update) | async-done | bytes 3317776 | tf_op jit(solution)/shard_map/all_gather | solution.py:190
  500.8 5.6 reshape.473
  511.7 19.8 fusion.144
  541.3 5.5 convert_element_type.183
  556.2 5.5 convert_element_type.190
  568.7 250.4 %all-reduce.16.cloned.1.call-done = (bf16[4,3,180,768]{3,0,1,2:T(4,128)(2,1)}, bf16[4,3,180,768]{3,0,1,2:T(4,128)(2,1)}) async-done(((bf16[4,3,180,768]{3,0,1,2:T(4,128)(2,1)}, bf16[4,3,180,768]{3,0,1,2:T(4,128)(2,1)}), (bf16[4,3,180,768]{3,0,1,2:T(4,128)(2,1)}, bf16[4,3,180,768]{3,0,1,2:T(4,128)(2,1)})) %all-reduce.16.cloned.1.call-update) | async-done | bytes 6635536
  826.1 12.6 copy.292
  838.7 14.7 reshape.515
  853.5 131.1 %reduce-scatter.9.cloned.1.call-done = f32[192,2304]{1,0:T(8,128)} async-done(((f32[768,2304]{1,0:T(8,128)}), f32[192,2304]{1,0:T(8,128)}) %reduce-scatter.9.cloned.1.call-update) | async-done | bytes 1769488
  994.1 7.5 all-to-all-start.2
  1001.9 7.5 fusion.58
  1013.8 6.2 all-to-all-done.2
  1040.8 23.7 %all_to_all.73 = bf16[4,96,2,3,192]{4,2,3,0,1:T(2,128)(2,1)S(1)} all-to-all(bf16[4,96,2,3,192]{4,2,3,0,1:T(2,128)(2,1)} %copy.200), channel_id=1, replica_groups=mesh['dp'=2,'wide'=32,'mlp'=4] {'wide'}, dimensions={1} | all-to-all | bytes 1769472 | tf_op jit(solution)/shard_map/all_to_all | solution.py:269
  1074.3 527.0 %all-reduce.14.cloned.1.call-done = (f32[2,2,96,96]{3,2,1,0:T(8,128)}, f32[2,2,96,96]{3,2,1,0:T(8,128)}, f32[768,768]{1,0:T(8,128)}, f32[768,768]{1,0:T(8,128)}) async-done(((f32[2,2,96,96]{3,2,1,0:T(8,128)}, f32[2,2,96,96]{3,2,1,0:T(8,128)}, f32[768,768]{1,0:T(8,128)}, f32[768,768]{1,0:T(8,128)}), (f32[2,2,96,96]{3,2,1,0:T(8,128)}, f32[2,2,96,96]{3,2,1,0:T(8,128)}, f32[768,768]{1,0:T(8,128)}, ...) | async-done | bytes 5013520 | tf_op jit(solution)/shard_map/psum | solution.py:292
  1601.3 20.1 all_gather.28
  1621.4 39.2 %all_gather.30 = f32[2,8,96,96]{3,2,1,0:T(8,128)} all-gather(f32[2,2,96,96]{3,2,1,0:T(8,128)} %get-tuple-element.87), channel_id=1, replica_groups=mesh['dp'=2,'wide'=32,'mlp'=4] {'mlp'}, dimensions={1}, use_global_device_ids=true | all-gather | bytes 737280 | tf_op jit(solution)/shard_map/all_gather | solution.py:312
  1660.7 52.4 %all-gather.11.cloned.1.call-done = bf16[4,3,2,96,768]{3,0,2,1,4:T(4,128)(2,1)} async-done(((bf16[4,3,2,96,192]{3,0,2,1,4:T(4,128)(2,1)}), bf16[4,3,2,96,768]{3,0,2,1,4:T(4,128)(2,1)}) %all-gather.11.cloned.1.call-update) | async-done | bytes 3538960 | tf_op jit(solution)/shard_map/all_gather | solution.py:272
  1713.1 6.2 fusion.46
  1719.4 14.1 all-reduce.9
  1733.8 273.3 %all-reduce.7 = (f32[192]{0:T(256)}, f32[192]{0:T(256)}, f32[2,2,96]{2,0,1:T(2,128)S(1)}, f32[2,2,96]{2,0,1:T(2,128)S(1)}, f32[192]{0:T(256)}, /*index=5*/f32[192]{0:T(256)}, f32[768]{0:T(1024)}, f32[192]{0:T(256)}) all-reduce(f32[192]{0:T(256)S(1)} %dynamic-slice.5, ...), channel_id=1, replica_groups=mesh['dp'=2,'wide'=32,'mlp'=4] {'dp','wide'}, use_global_device_ids=true, to_apply=%region_14.15 | all-reduce | flops 2496 | bytes 19968 | tf_op jit(solution)/shard_map/psum | solution.py:292
  2007.1 11.0 all_gather.29
  2018.7 9.9 all_gather.31
  (249 shorter events, 158.2 us)
Async XLA Ops:
  7.2 504.4 %copy-start = (bf16[768,768]{1,0:T(8,128)(2,1)S(1)}, bf16[768,768]{1,0:T(8,128)(2,1)}, u32[]{:S(2)}) copy-start(bf16[768,768]{1,0:T(8,128)(2,1)} %param.27) | copy-start | bytes 3538948
  7.2 170.7 %reduce-scatter.7.cloned.1.call-start = ((), (), s32[]{:S(2)}) async-start(), calls=%async_computation.10 | async-start | bytes 8847360
  8.1 338.8 %copy-start.31 = (f32[4,3,45]{2,1,0:T(4,128)}, f32[4,3,45]{2,1,0:T(4,128)S(1)}, u32[]{:S(2)}) copy-start(f32[4,3,45]{2,1,0:T(4,128)S(1)} %copy.161) | copy-start | bytes 6484
  9.5 337.4 %copy-start.33 = (f32[4,3,45]{2,1,0:T(4,128)}, f32[4,3,45]{2,1,0:T(4,128)S(1)}, u32[]{:S(2)}) copy-start(f32[4,3,45]{2,1,0:T(4,128)S(1)} %broadcast_multiply_fusion.5) | copy-start | bytes 6484
  11.0 335.8 %copy-start.39 = (f32[4,3,45]{2,1,0:T(4,128)}, f32[4,3,45]{2,1,0:T(4,128)S(1)}, u32[]{:S(2)}) copy-start(f32[4,3,45]{2,1,0:T(4,128)S(1)} %add_rsqrt_fusion.2) | copy-start | bytes 6484
  190.0 26.8 %all-to-all-start = ((bf16[4,3,2,96,192]{4,0,2,1,3:T(4,128)(2,1)}), bf16[4,3,2,96,192]{4,0,2,1,3:T(4,128)(2,1)}, u32[]{:S(2)}, u32[]{:S(2)}) async-start(bf16[4,3,2,96,192]{4,0,2,1,3:T(4,128)(2,1)} %copy.162), calls=%async_computation | async-start | bytes 2359296 | tf_op jit(solution)/shard_map/all_to_all | solution.py:149
  198.3 148.5 %all-gather.5.cloned.1.call-start = ((), (), s32[]{:S(2)}) async-start(), calls=%async_computation.6 | async-start | bytes 5898240 | tf_op jit(solution)/shard_map/all_gather | solution.py:177
  269.0 77.9 %copy-start.50 = (f32[768]{0:T(1024)S(1)}, f32[768]{0:T(1024)}, u32[]{:S(2)}) copy-start(f32[768]{0:T(1024)} %param.17) | copy-start | bytes 9220
  269.0 77.9 %copy-start.55 = (f32[768]{0:T(1024)S(1)}, f32[768]{0:T(1024)}, u32[]{:S(2)}) copy-start(f32[768]{0:T(1024)} %param.18) | copy-start | bytes 9220
  269.0 155.1 %all-gather.9.cloned.1.call-start = ((), (), s32[]{:S(2)}) async-start(), calls=%async_computation.8 | async-start | bytes 4147200 | tf_op jit(solution)/shard_map/all_gather | solution.py:191
  271.3 225.4 %all-gather.7.cloned.1.call-start = ((), (), s32[]{:S(2)}) async-start(), calls=%async_computation.7 | async-start | bytes 4147200 | tf_op jit(solution)/shard_map/all_gather | solution.py:190
  354.2 464.8 %all-reduce.16.cloned.1.call-start = ((), (), s32[]{:S(2)}) async-start(), calls=%async_computation.13 | async-start | bytes 13271040
  566.8 255.3 %copy-start.7 = (bf16[4,3,45,768]{3,0,2,1:T(4,128)(2,1)S(1)}, bf16[4,3,45,768]{3,0,2,1:T(4,128)(2,1)}, u32[]{:S(2)}) copy-start(bf16[4,3,45,768]{3,0,2,1:T(4,128)(2,1)} %param.29) | copy-start | bytes 2488324
  566.8 417.8 %reduce-scatter.9.cloned.1.call-start = ((), (), s32[]{:S(2)}) async-start(), calls=%async_computation.11 | async-start | bytes 8847360
  994.1 25.9 %all-to-all-start.2 = ((bf16[4,3,2,96,192]{4,0,2,1,3:T(4,128)(2,1)}), bf16[4,3,2,96,192]{4,0,2,1,3:T(4,128)(2,1)S(1)}, u32[]{:S(2)}, u32[]{:S(2)}) async-start(bf16[4,3,2,96,192]{4,0,2,1,3:T(4,128)(2,1)} %copy.186), calls=%async_computation.2 | async-start | bytes 2359296 | tf_op jit(solution)/shard_map/all_to_all | solution.py:234
  1001.6 599.7 %all-reduce.14.cloned.1.call-start = ((), (), s32[]{:S(2)}) async-start(), calls=%async_computation.12 | async-start | bytes 10223616 | tf_op jit(solution)/shard_map/psum | solution.py:292
  1036.5 676.6 %all-gather.11.cloned.1.call-start = ((), (), s32[]{:S(2)}) async-start(), calls=%async_computation.9 | async-start | bytes 5898240 | tf_op jit(solution)/shard_map/all_gather | solution.py:272
  1072.9 640.2 %copy-start.2 = (bf16[4,3,45,768]{3,0,2,1:T(4,128)(2,1)S(1)}, bf16[4,3,45,768]{3,0,2,1:T(4,128)(2,1)}, u32[]{:S(2)}) copy-start(bf16[4,3,45,768]{3,0,2,1:T(4,128)(2,1)} %param.15) | copy-start | bytes 2488324
  1072.9 640.2 %copy-start.28 = (bf16[180,1,96]{2,0,1:T(8,128)(2,1)S(1)}, bf16[180,1,96]{2,0,1:T(8,128)(2,1)}, u32[]{:S(2)}) copy-start(bf16[180,1,96]{2,0,1:T(8,128)(2,1)} %copy-done.27) | copy-start | bytes 103684
  1072.9 640.2 %copy-start.30 = (bf16[180,1,96]{2,0,1:T(8,128)(2,1)S(1)}, bf16[180,1,96]{2,0,1:T(8,128)(2,1)}, u32[]{:S(2)}) copy-start(bf16[180,1,96]{2,0,1:T(8,128)(2,1)} %copy-done.29) | copy-start | bytes 103684
  1072.9 640.2 %copy-start.34 = (f32[4,3,45]{2,1,0:T(4,128)S(1)}, f32[4,3,45]{2,1,0:T(4,128)}, u32[]{:S(2)}) copy-start(f32[4,3,45]{2,1,0:T(4,128)} %copy-done.33) | copy-start | bytes 6484
  1072.9 640.2 %copy-start.40 = (f32[4,3,45]{2,1,0:T(4,128)S(1)}, f32[4,3,45]{2,1,0:T(4,128)}, u32[]{:S(2)}) copy-start(f32[4,3,45]{2,1,0:T(4,128)} %copy-done.39) | copy-start | bytes 6484
  1072.9 640.2 %copy-start.42 = (f32[4,3,45]{2,1,0:T(4,128)S(1)}, f32[4,3,45]{2,1,0:T(4,128)}, u32[]{:S(2)}) copy-start(f32[4,3,45]{2,1,0:T(4,128)} %copy-done.41) | copy-start | bytes 6484
  1072.9 640.2 %copy-start.44 = (f32[4,3,45]{2,1,0:T(4,128)S(1)}, f32[4,3,45]{2,1,0:T(4,128)}, u32[]{:S(2)}) copy-start(f32[4,3,45]{2,1,0:T(4,128)} %copy-done.43) | copy-start | bytes 6484
  1072.9 640.2 %copy-start.46 = (f32[768]{0:T(1024)S(1)}, f32[768]{0:T(1024)}, u32[]{:S(2)}) copy-start(f32[768]{0:T(1024)} %param.23) | copy-start | bytes 9220
  1073.0 640.2 %copy-start.51 = (f32[768]{0:T(1024)S(1)}, f32[768]{0:T(1024)}, u32[]{:S(2)}) copy-start(f32[768]{0:T(1024)} %param.17) | copy-start | bytes 9220
  1660.6 58.7 %copy-start.47 = (f32[768]{0:T(1024)S(1)}, f32[768]{0:T(1024)}, u32[]{:S(2)}) copy-start(f32[768]{0:T(1024)} %get-tuple-element.108) | copy-start | bytes 9220
  1660.6 58.7 %copy-start.48 = (f32[768]{0:T(1024)S(1)}, f32[768]{0:T(1024)}, u32[]{:S(2)}) copy-start(f32[768]{0:T(1024)} %get-tuple-element.74) | copy-start | bytes 9220
  1660.6 58.7 %copy-start.49 = (f32[768]{0:T(1024)S(1)}, f32[768]{0:T(1024)}, u32[]{:S(2)}) copy-start(f32[768]{0:T(1024)} %get-tuple-element.77) | copy-start | bytes 9220
  1660.6 73.2 %copy-start.52 = (f32[2,2,96]{2,0,1:T(2,128)S(1)}, f32[2,2,96]{2,0,1:T(2,128)}, u32[]{:S(2)}) copy-start(f32[2,2,96]{2,0,1:T(2,128)} %get-tuple-element.104) | copy-start | bytes 4612
  1660.6 73.2 %copy-start.58 = (f32[768]{0:T(1024)S(1)}, f32[768]{0:T(1024)}, u32[]{:S(2)}) copy-start(f32[768]{0:T(1024)} %get-tuple-element.97) | copy-start | bytes 9220
  1660.6 73.2 %copy-start.62 = (f32[2,2,96]{2,0,1:T(2,128)S(1)}, f32[2,2,96]{2,0,1:T(2,128)}, u32[]{:S(2)}) copy-start(f32[2,2,96]{2,0,1:T(2,128)} %get-tuple-element.106) | copy-start | bytes 4612
  (44 other events, 292.9 us)
Sparse Core Ops, SparseCore 0:
  43.7 134.2 reduce-scatter.6
  269.1 77.6 all-gather.4
  349.3 74.8 all-gather.8
  426.4 70.2 all-gather.6
  566.9 252.0 all-reduce.15
  853.6 130.9 reduce-scatter.8
  1036.6 564.6 all-reduce.13
  1603.7 109.3 all-gather.10
where the time goes:
time: 2060 us; the launch traced here: 2050 us
  waiting for transfers between devices  1330 us (65%)
  blocking collectives  414 us (20%)
  local copies, waits for them, and re-layouts  167 us (8%)
  matrix products  78.4 us (4%)
  other arithmetic  28.5 us (1%)
    psum x1, waiting for transfers between devices, shards(): lax.psum((grad_weight_in, grad_bias_in, grad_weight_out, small[4], small[...  527 us
    unnamed x11, waiting for transfers between devices  515 us
    psum x1, blocking collectives, shards(): lax.psum((grad_weight_in, grad_bias_in, grad_weight_out, small[4], small[...  273 us
    unnamed x158, local copies, waits for them, and re-layouts  90 us
    all_gather x1, waiting for transfers between devices, shards(): whole_spec = lax.all_gather(returned, 'mlp', axis=4, tiled=True)  75.1 us
    all_gather x1, waiting for transfers between devices, shards(): lax.all_gather(grad_branch.astype(jnp.bfloat16), 'mlp', axis=2, tiled=True)  69.9 us
    all_gather x1, waiting for transfers between devices, shards(): lax.all_gather(mixed_low, 'mlp', axis=2, tiled=True)  62.7 us
    all_gather x1, waiting for transfers between devices, shards(): whole_grad = lax.all_gather(grad_row_spectrum, 'mlp', axis=4, tiled=True)  52.4 us
  transfers between devices with their start and end apart: 10, of which 10 were waited for; matrix products, arithmetic and copies ran while one was open for 2% of the time, Pallas kernels for 0%

commit v1 on v0

v1 whole, which is shorter than its diff:
```python
import math

import jax
import jax.numpy as jnp
import numpy as np
from jax import lax
from jax.sharding import Mesh
from jax.sharding import PartitionSpec as P

H = 96
KWP = 96
W = 180
WPAD = 48
EPSILON = 1e-05
SHRINK = 0.01

XY = ("x", "y")
WIDE = ("x", "y", "core")
PAIR = ("core", "mlp")
ZED = ("dp", "mlp")
EVERY = ("dp", "x", "y", "core", "mlp")
bf16 = jnp.bfloat16
f32 = jnp.float32


def tables():
    w = np.arange(W)
    k = np.arange(KWP)
    phase = 2.0 * np.pi * ((w[:, None] * k[None, :]) % W) / W
    live = np.where(k < W // 2 + 1, 1.0 / math.sqrt(W), 0.0)
    weight = np.where((k == 0) | (2 * k == W), 1.0, 2.0) * live
    fwd = np.stack([np.cos(phase) * live, -np.sin(phase) * live], axis=2)
    inv = np.stack([np.cos(phase) * weight, -np.sin(phase) * weight], axis=2)
    pad = ((0, 0), (0, WPAD - W // 4), (0, 0), (0, 0))
    fwd = np.pad(fwd.reshape(4, W // 4, KWP, 2), pad).reshape(4, WPAD, 16, 6, 2)
    inv = np.pad(inv.reshape(4, W // 4, KWP, 2), pad).reshape(4, WPAD, 16, 6, 2)
    same = np.eye(6).reshape(2, 3, 6)
    lon_fwd = np.einsum("mwqkp,rih->qhkprmiw", fwd, same).reshape(1152, 1152)
    lon_inv = np.einsum("mwqkp,rih->qhkprmiw", inv, same).reshape(1152, 1152)
    h = np.arange(H)
    angle = 2.0 * np.pi * ((h[:, None] * h[None, :]) % H) / H
    cos = np.cos(angle) / math.sqrt(H)
    sin = np.sin(angle) / math.sqrt(H)
    lat_fwd = np.stack([np.stack([cos, sin]), np.stack([-sin, cos])])
    lat_inv = np.stack([np.stack([cos, -sin]), np.stack([sin, cos])])
    kk = np.eye(6)
    grid_fwd = np.einsum(
        "pqjah,kl->pkjahlq", lat_fwd.reshape(2, 2, H, 16, 6), kk
    ).reshape(1152, 1152)
    grid_inv = np.einsum(
        "pqahj,kl->ahkpqlj", lat_inv.reshape(2, 2, 16, 6, H), kk
    ).reshape(1152, 1152)
    return tuple(np.asarray(t, np.float32).astype(bf16) for t in (lon_fwd, lon_inv, grid_fwd, grid_inv))


def shrink(value):
    return value - SHRINK * value * lax.rsqrt(value * value + SHRINK * SHRINK)


def shrink_slope(value):
    inverse_root = lax.rsqrt(value * value + SHRINK * SHRINK)
    return 1.0 - SHRINK * SHRINK * SHRINK * inverse_root * inverse_root * inverse_root


def gelu_exact(value):
    return jax.nn.gelu(value, approximate=False)


def gelu_back(value, grad):
    return jax.vjp(gelu_exact, value)[1](grad)[0]


def mm(left, right):
    return jnp.dot(left, right, preferred_element_type=f32)


def inner_rows(left, right):
    return lax.dot_general(left, right, (((0,), (0,)), ((), ())), preferred_element_type=f32)


def outer_cols(left, right):
    return lax.dot_general(left, right, (((1,), (1,)), ((), ())), preferred_element_type=f32)


def swap(value, axes):
    return lax.all_to_all(value, axes, 0, 0, tiled=True)


def spread(value, axes, count):
    return swap(jnp.broadcast_to(value[None], (count,) + value.shape), axes)


def block_form(weights):
    eye = jnp.eye(4, dtype=weights.dtype)
    dense = jnp.einsum("pbef,bc->pbecf", weights, eye).reshape(2, 384, 384)
    return jnp.concatenate(
        [
            jnp.concatenate([dense[0], dense[1]], axis=1),
            jnp.concatenate([-dense[1], dense[0]], axis=1),
        ],
        axis=0,
    )


def block_grads(grad):
    quad = grad.reshape(2, 384, 2, 384)
    real = quad[0, :, 0] + quad[1, :, 1]
    imag = quad[0, :, 1] - quad[1, :, 0]
    both = jnp.stack([real, imag])
    return jnp.stack([both[:, 96 * b : 96 * b + 96, 96 * b : 96 * b + 96] for b in range(4)], axis=1)


def pack(tokens):
    halves = jnp.stack([tokens[..., :384], tokens[..., 384:]])
    return swap(halves.reshape(8, 144, 384), PAIR).reshape(1152, 384)


def unpack(rows):
    back = swap(rows.reshape(8, 144, 384), PAIR).reshape(2, 4, 3, WPAD, 384)
    return jnp.concatenate([back[0], back[1]], axis=-1)


def across(rows):
    return swap(rows.reshape(16, 72, 384), XY).reshape(1152, 384)


def lanes(rows):
    return jnp.concatenate([rows[:576], rows[576:]], axis=1)


def unlanes(wide_rows):
    return jnp.concatenate([wide_rows[:, :384], wide_rows[:, 384:]], axis=0)


def shards(
    inputs,
    validity,
    gain_first,
    shift_first,
    spectral_in,
    spectral_in_bias,
    spectral_out,
    spectral_out_bias,
    gain_second,
    shift_second,
    weight_in,
    bias_in,
    weight_out,
    bias_out,
    cotangent,
):
    half = lax.axis_index("core")
    group = lax.axis_index("mlp")
    wide = lax.axis_index(WIDE)
    lon_fwd, lon_inv, grid_fwd, grid_inv = (jnp.asarray(t) for t in tables())

    both = jnp.concatenate([weight_in, weight_out], axis=0)
    piece = lax.dynamic_slice_in_dim(both, wide * 48, 48, 0)
    parts = spread(
        jnp.concatenate([piece, spectral_in.reshape(48, 768), spectral_out.reshape(48, 768)]),
        "mlp",
        4,
    )
    vectors = spread(
        jnp.concatenate([bias_in, spectral_in_bias.reshape(-1), spectral_out_bias.reshape(-1)]).reshape(
            12, 128
        ),
        "mlp",
        4,
    ).reshape(4, 1536)
    whole = lax.all_gather(parts[:, :48], WIDE)
    w_in = [whole[:16, g].reshape(768, 768) for g in range(4)]
    w_out = [whole[16:, g].reshape(768, 768) for g in range(4)]
    units = vectors[:, :768]

    def my_half(value):
        value = lax.dynamic_slice_in_dim(value, half * 2, 2, 0).swapaxes(0, 1)
        return value.reshape((2, 4) + value.shape[3:])

    mix_in = block_form(my_half(parts[:, 48:96].reshape(4, 2, 2, 96, 96)))
    mix_out = block_form(my_half(parts[:, 96:].reshape(4, 2, 2, 96, 96)))
    mix_in_bias = my_half(vectors[:, 768:1152].reshape(4, 2, 2, 96)).reshape(768)
    mix_out_bias = my_half(vectors[:, 1152:].reshape(4, 2, 2, 96)).reshape(768)

    def widen(value):
        return jnp.pad(value, ((0, 0), (0, 0), (0, WPAD - W // 4), (0, 0)))

    resid = widen(inputs).astype(f32)
    present = widen(validity.astype(f32)[..., None])
    centred_first = resid - jnp.mean(resid, axis=3, keepdims=True)
    scale_first = lax.rsqrt(
        jnp.mean(centred_first * centred_first, axis=3, keepdims=True) + EPSILON
    )
    normed_first = centred_first * scale_first
    masked = (normed_first * gain_first + shift_first) * present

    spectrum = mm(lon_fwd, pack(masked.astype(bf16))).astype(bf16)
    columns = across(spectrum)
    grid_low = lanes(mm(grid_fwd, columns).astype(bf16))
    first_layer = mm(grid_low, mix_in) + mix_in_bias
    active = gelu_exact(first_layer).astype(bf16)
    second = mm(active, mix_out) + mix_out_bias
    shrunk = unlanes(shrink(second).astype(bf16))
    back_low = mm(grid_inv, shrunk).astype(bf16)
    returned = across(back_low)
    filtered = unpack(inner_rows(lon_inv, returned).astype(bf16)).astype(f32)

    stream = resid + filtered + masked
    stream_low = stream.astype(bf16).astype(f32)
    centred = stream_low - jnp.mean(stream_low, axis=3, keepdims=True)
    scale_second = lax.rsqrt(jnp.mean(centred * centred, axis=3, keepdims=True) + EPSILON)
    normed_second = centred * scale_second
    mixed_low = (normed_second * gain_second + shift_second).astype(bf16)
    grad_output = widen(cotangent).astype(f32)
    grad_branch = grad_output * present
    mixed_rows = mixed_low.reshape(576, 768)
    grad_rows = grad_branch.astype(bf16).reshape(576, 768)

    branch = jnp.zeros((576, 768), f32)
    grad_mixed = jnp.zeros((576, 768), f32)
    hidden = []
    grad_pre_low = []
    grad_bias_in = []
    for g in range(4):
        pre_act = mm(mixed_rows, w_in[g]) + units[g]
        grad_pre = gelu_back(pre_act, outer_cols(grad_rows, w_out[g]))
        grad_bias_in.append(jnp.sum(grad_pre, axis=0))
        grad_pre_low.append(grad_pre.astype(bf16))
        grad_mixed = grad_mixed + outer_cols(grad_pre_low[g], w_in[g]).astype(bf16).astype(f32)
        hidden.append(gelu_exact(pre_act).astype(bf16))
        branch = branch + mm(hidden[g], w_out[g]).astype(bf16).astype(f32)
    branch = branch.reshape(4, 3, WPAD, 768) + bias_out
    output = (stream + present * branch).astype(bf16)[:, :, : W // 4]

    grad_bias_out = jnp.sum(grad_branch, axis=(0, 1, 2))
    grad_norm = grad_mixed.reshape(4, 3, WPAD, 768)
    grad_gain_second = jnp.sum(grad_norm * normed_second, axis=(0, 1, 2))
    grad_shift_second = jnp.sum(grad_norm, axis=(0, 1, 2))
    scaled = grad_norm * gain_second
    grad_stream = grad_output + scale_second * (
        scaled
        - jnp.mean(scaled, axis=3, keepdims=True)
        - normed_second * jnp.mean(scaled * normed_second, axis=3, keepdims=True)
    )

    grad_weights = jnp.stack(
        [
            jnp.concatenate(
                [inner_rows(mixed_rows, grad_pre_low[g]), inner_rows(hidden[g], grad_rows)], axis=0
            ).astype(bf16)
            for g in range(4)
        ]
    )
    grad_weights = grad_weights.reshape(4, 32, 48, 768).swapaxes(0, 1).reshape(6144, 768)
    share = lax.psum_scatter(grad_weights, WIDE, scatter_dimension=0, tiled=True)
    share = share.reshape(4, 48, 768)
    share = swap(jnp.concatenate([share, share], axis=0), ZED)
    share = jnp.sum(share.astype(f32), axis=0).astype(bf16)
    grad_slices = lax.all_gather(share, WIDE).reshape(1536, 768).astype(f32)

    def total(vector):
        near = jnp.sum(spread(vector, ("dp", "core", "mlp"), 16), axis=0)
        return jnp.sum(spread(near, XY, 16), axis=0)

    early = total(
        jnp.concatenate(grad_bias_in + [grad_bias_out, grad_gain_second, grad_shift_second]).reshape(
            42, 128
        )
    ).reshape(7, 768)

    grad_back = mm(lon_inv, pack(grad_stream.astype(bf16))).astype(bf16)
    grad_columns = across(grad_back)
    grad_shrunk = lanes(inner_rows(grid_inv, grad_columns))
    grad_second = grad_shrunk * shrink_slope(second)
    grad_second_low = grad_second.astype(bf16)
    grad_first = gelu_back(first_layer, outer_cols(grad_second_low, mix_out))
    grad_first_low = grad_first.astype(bf16)
    grad_grid = unlanes(outer_cols(grad_first_low, mix_in).astype(bf16))
    grad_spectrum = inner_rows(grid_fwd, grad_grid).astype(bf16)
    grad_from_spec = unpack(inner_rows(lon_fwd, across(grad_spectrum)).astype(bf16)).astype(f32)

    grad_filters = jnp.stack(
        [
            block_grads(inner_rows(grid_low, grad_first_low)),
            block_grads(inner_rows(active, grad_second_low)),
        ]
    ).astype(bf16)
    filters = swap(grad_filters.reshape(16, 72, 128), XY)
    filters = jnp.sum(filters.astype(f32), axis=0).astype(bf16)
    filters = jnp.sum(spread(filters, ZED, 8).astype(f32), axis=0).astype(bf16)
    filters = spread(filters, WIDE, 32).reshape(16, 2, 9216).swapaxes(0, 1).astype(f32)
    filters = filters.reshape(2, 2, 2, 4, 96, 96).transpose(1, 2, 0, 3, 4, 5)
    filters = filters.reshape(2, 2, 8, 96, 96)

    grad_normed = (grad_from_spec + grad_stream) * present
    grad_gain_first = jnp.sum(grad_normed * normed_first, axis=(0, 1, 2))
    grad_shift_first = jnp.sum(grad_normed, axis=(0, 1, 2))
    scaled_first = grad_normed * gain_first
    grad_inputs = grad_stream + scale_first * (
        scaled_first
        - jnp.mean(scaled_first, axis=3, keepdims=True)
        - normed_first * jnp.mean(scaled_first * normed_first, axis=3, keepdims=True)
    )
    grad_inputs = grad_inputs[:, :, : W // 4]

    filter_bias = jnp.stack([jnp.sum(grad_first, axis=0), jnp.sum(grad_second, axis=0)])
    filter_bias = filter_bias.reshape(2, 2, 1, 384)
    filter_bias = jnp.where(
        half == jnp.arange(2, dtype=jnp.int32)[None, None, :, None], filter_bias, 0.0
    ).reshape(3072)
    late = total(
        jnp.concatenate([grad_gain_first, grad_shift_first, filter_bias]).reshape(36, 128)
    ).reshape(6, 768)
    filter_bias = late[2:].reshape(2, 2, 8, 96)

    def mine(vector):
        return lax.dynamic_slice_in_dim(vector, group * 192, 192, 0)

    return (
        output,
        grad_inputs,
        mine(late[0]),
        mine(late[1]),
        filters[0],
        filter_bias[0],
        filters[1],
        filter_bias[1],
        mine(early[5]),
        mine(early[6]),
        grad_slices[:768],
        lax.dynamic_slice_in_dim(early[:4], group, 1, 0)[0],
        grad_slices[768:],
        mine(early[4]),
    )


def solution(mesh):
    fine = Mesh(mesh.devices.reshape(2, 4, 4, 2, 4), EVERY)
    tokens = P("dp", WIDE, "mlp")
    placed = (
        tokens,
        tokens,
        P(),
        P(),
        P(None, "mlp"),
        P(None, "mlp"),
        P(None, "mlp"),
        P(None, "mlp"),
        P(),
        P(),
        P(None, "mlp"),
        P("mlp"),
        P("mlp", None),
        P(),
        tokens,
    )
    return jax.shard_map(
        shards,
        mesh=fine,
        in_specs=placed,
        out_specs=(
            tokens,
            tokens,
            P("mlp"),
            P("mlp"),
            P(),
            P(),
            P(),
            P(),
            P("mlp"),
            P("mlp"),
            P(None, "mlp"),
            P("mlp"),
            P("mlp", None),
            P("mlp"),
        ),
        check_vma=False,
    )
```

time: 2060 us -> 540 us (0.26)
  waiting for transfers between devices: 1330 us -> 108 us
  blocking collectives: 414 us -> 102 us
  local copies, waits for them, and re-layouts: 167 us -> 89.1 us
  starting transfers between devices: 17.2 us -> 84 us
    psum x1 -> x0, waiting for transfers between devices: 527 us -> none  [shards(): lax.psum((grad_weight_in, grad_bias_in, grad_weight_out, small[4], small[...]
    unnamed x11 -> x3, waiting for transfers between devices: 515 us -> 0.05 us
    psum x1 -> x0, blocking collectives: 273 us -> none  [shards(): lax.psum((grad_weight_in, grad_bias_in, grad_weight_out, small[4], small[...]
    all_gather x4 -> x2, waiting for transfers between devices: 260 us -> 0.01 us  [the longest x1 0.01 us: shards(): whole = lax.all_gather(parts[:, :48], WIDE)]
    all_to_all x2 -> x14, waiting for transfers between devices: 23.9 us -> 108 us  [swap(): return lax.all_to_all(value, axes, 0, 0, tiled=True)]
    all_gather x4 -> x0, blocking collectives: 80.2 us -> none  [the longest x1 39.2 us: shards(): lax.all_gather(summed[10], 'mlp', axis=1, tiled=True)]
    unnamed x158 -> x225, local copies, waits for them, and re-layouts: 90 us -> 15.6 us
    all_to_all x2 -> x14, starting transfers between devices: 15.9 us -> 84 us  [swap(): return lax.all_to_all(value, axes, 0, 0, tiled=True)]
  transfers between devices with their start and end apart: 10 -> 17, of which waited for: 10 -> 14; matrix products, arithmetic and copies ran while one was open for 2% -> 30% of each run, Pallas kernels for 0% -> 0%
where the time goes in v1:
time: 540 us; the launch traced here: 533 us
  waiting for transfers between devices  108 us (20%)
  blocking collectives  102 us (19%)
  matrix products  98 us (18%)
  local copies, waits for them, and re-layouts  89.1 us (16%)
  starting transfers between devices  84 us (16%)
  other arithmetic  35.4 us (7%)
  between operations  15.8 us (3%)
    all_to_all x14, waiting for transfers between devices, swap(): return lax.all_to_all(value, axes, 0, 0, tiled=True)  108 us
    all_to_all x4, blocking collectives, swap(): return lax.all_to_all(value, axes, 0, 0, tiled=True)  102 us
    all_to_all x14, starting transfers between devices, swap(): return lax.all_to_all(value, axes, 0, 0, tiled=True)  84 us
    dot_general x15, matrix products, mm(): return jnp.dot(left, right, preferred_element_type=f32)  36.1 us
    dot_general x10, matrix products, outer_cols(): lax.dot_general(left, right, (((1,), (1,)), ((), ())), preferred_element_...  32.9 us
    dot_general x15, matrix products, inner_rows(): lax.dot_general(left, right, (((0,), (0,)), ((), ())), preferred_element_...  28.9 us
    unnamed x225, local copies, waits for them, and re-layouts  15.6 us
  transfers between devices with their start and end apart: 17, of which 14 were waited for; matrix products, arithmetic and copies ran while one was open for 30% of the time, Pallas kernels for 0%

profile of v1, /device:TPU:1, one launch (start us, length us, event | category | flops | bytes accessed | tf_op | source)
XLA Modules:
  0.0 532.8 jit_solution(6518819041327332035)
XLA Ops:
  10.4 30.8 %all_to_all.90 = bf16[4,144,768]{2,1,0:T(8,128)(2,1)S(1)} all-to-all(bf16[4,144,768]{2,1,0:T(8,128)(2,1)S(1)} %broadcast_in_dim.38), channel_id=1, replica_groups=mesh['dp'=2,'x'=4,'y'=4,'core'=2,'mlp'=4] {'mlp'}, dimensions={0} | all-to-all | bytes 1769472 | tf_op jit(solution)/shard_map/all_to_all | solution.py:86
  43.0 4.6 all-to-all-start.3
  50.0 4.4 all-to-all-done.3
  54.4 8.1 %all-to-all-start = ((bf16[8,144,384]{2,1,0:T(8,128)(2,1)}), bf16[8,144,384]{2,1,0:T(8,128)(2,1)}, u32[]{:S(2)}, u32[]{:S(2)}) async-start(bf16[8,144,384]{2,1,0:T(8,128)(2,1)} %bitcast.4), calls=%async_computation | async-start | bytes 1769472 | tf_op jit(solution)/shard_map/all_to_all | solution.py:86
  78.0 7.2 %all-to-all-done = bf16[8,144,384]{2,1,0:T(8,128)(2,1)} async-done(((bf16[8,144,384]{2,1,0:T(8,128)(2,1)}), bf16[8,144,384]{2,1,0:T(8,128)(2,1)}, u32[]{:S(2)}, u32[]{:S(2)}) %all-to-all-start) | async-done | bytes 884768 | tf_op jit(solution)/shard_map/all_to_all | solution.py:86
  91.1 7.2 %all-to-all-start.1 = ((bf16[16,72,384]{2,1,0:T(8,128)(2,1)}), bf16[16,72,384]{2,1,0:T(8,128)(2,1)}, u32[]{:S(2)}, u32[]{:S(2)}) async-start(bf16[16,72,384]{2,1,0:T(8,128)(2,1)} %bitcast.7), calls=%async_computation.1 | async-start | bytes 1769472 | tf_op jit(solution)/shard_map/all_to_all | solution.py:86
  101.8 10.7 %all-to-all-done.1 = bf16[16,72,384]{2,1,0:T(8,128)(2,1)} async-done(((bf16[16,72,384]{2,1,0:T(8,128)(2,1)}), bf16[16,72,384]{2,1,0:T(8,128)(2,1)}, u32[]{:S(2)}, u32[]{:S(2)}) %all-to-all-start.1) | async-done | bytes 884768 | tf_op jit(solution)/shard_map/all_to_all | solution.py:86
  116.6 9.9 %multiply_convert_fusion.4 = (bf16[576,768]{1,0:T(8,128)(2,1)S(1)}, f32[576,768]{1,0:T(8,128)}, f32[576,768]{1,0:T(8,128)}) fusion(f32[768]{0:T(1024)S(1)} %copy-done.86, bf16[384,384]{1,0:T(8,128)(2,1)S(1)} %squeeze.66, bf16[384,384]{1,0:T(8,128)(2,1)S(1)} %neg.46, bf16[384,384]{1,0:T(8,128)(2,1)S(1)} %squeeze.67, ...), kind=kOutput, calls=%fused_computation.136 | convolution fusion | flops 715161600 | bytes 6196224 | tf_op jit(solution)/shard_map/dot_general | solution.py:74
  132.0 17.2 %all_to_all.91 = bf16[16,72,384]{2,1,0:T(8,128)(2,1)S(1)} all-to-all(bf16[16,72,384]{2,1,0:T(8,128)(2,1)S(1)} %bitcast.271), channel_id=1, replica_groups=mesh['dp'=2,'x'=4,'y'=4,'core'=2,'mlp'=4] {'x','y'}, dimensions={0} | all-to-all | bytes 1769472 | tf_op jit(solution)/shard_map/all_to_all | solution.py:86
  153.8 10.5 %all-to-all-start.5 = ((bf16[8,144,384]{2,1,0:T(8,128)(2,1)}), bf16[8,144,384]{2,1,0:T(8,128)(2,1)S(1)}, u32[]{:S(2)}, u32[]{:S(2)}) async-start(bf16[8,144,384]{2,1,0:T(8,128)(2,1)} %bitcast.25), calls=%async_computation.5 | async-start | bytes 1769472 | tf_op jit(solution)/shard_map/all_to_all | solution.py:86
  165.1 22.7 %all-to-all-done.5 = bf16[8,144,384]{2,1,0:T(8,128)(2,1)S(1)} async-done(((bf16[8,144,384]{2,1,0:T(8,128)(2,1)}), bf16[8,144,384]{2,1,0:T(8,128)(2,1)S(1)}, u32[]{:S(2)}, u32[]{:S(2)}) %all-to-all-start.5) | async-done | bytes 884768 | tf_op jit(solution)/shard_map/all_to_all | solution.py:86
  197.9 5.4 %fusion.122 = (f32[768]{0:T(1024)}, bf16[576,768]{1,0:T(8,128)(2,1)S(1)}, f32[576,768]{1,0:T(8,128)S(1)}) fusion(f32[576,768]{1,0:T(8,128)S(1)} %fusion.153, f32[768]{0:T(1024)S(1)} %copy-done.78, bf16[576,768]{1,0:T(8,128)(2,1)S(1)} %bitcast.296, bf16[768,768]{1,0:T(8,128)(2,1)S(1)} %bitcast.286), kind=kOutput, calls=%fused_computation.290 | convolution fusion | flops 712211712 | bytes 6494208 | tf_op jit(solution)/shard_map/dot_general | solution.py:82
  204.4 5.4 %fusion.124 = (f32[768]{0:T(1024)}, bf16[576,768]{1,0:T(8,128)(2,1)S(1)}, f32[576,768]{1,0:T(8,128)S(1)}) fusion(f32[576,768]{1,0:T(8,128)S(1)} %fusion.152, f32[768]{0:T(1024)S(1)} %copy-done.77, bf16[576,768]{1,0:T(8,128)(2,1)S(1)} %bitcast.297, bf16[768,768]{1,0:T(8,128)(2,1)S(1)} %bitcast.284), kind=kOutput, calls=%fused_computation.291 | convolution fusion | flops 712211712 | bytes 6494208 | tf_op jit(solution)/shard_map/dot_general | solution.py:82
  210.9 5.4 %fusion.126 = (f32[768]{0:T(1024)}, bf16[576,768]{1,0:T(8,128)(2,1)S(1)}, f32[576,768]{1,0:T(8,128)S(1)}) fusion(f32[576,768]{1,0:T(8,128)S(1)} %fusion.151, f32[768]{0:T(1024)S(1)} %copy-done.76, bf16[576,768]{1,0:T(8,128)(2,1)S(1)} %bitcast.298, bf16[768,768]{1,0:T(8,128)(2,1)S(1)} %bitcast.282), kind=kOutput, calls=%fused_computation.292 | convolution fusion | flops 712211712 | bytes 6494208 | tf_op jit(solution)/shard_map/dot_general | solution.py:82
  217.5 5.4 %fusion.128 = (f32[768]{0:T(1024)}, bf16[576,768]{1,0:T(8,128)(2,1)S(1)}, f32[576,768]{1,0:T(8,128)S(1)}) fusion(f32[576,768]{1,0:T(8,128)S(1)} %fusion.150, f32[768]{0:T(1024)S(1)} %copy-done.75, bf16[576,768]{1,0:T(8,128)(2,1)S(1)} %bitcast.299, bf16[768,768]{1,0:T(8,128)(2,1)S(1)} %bitcast.280), kind=kOutput, calls=%fused_computation.293 | convolution fusion | flops 712211712 | bytes 6494208 | tf_op jit(solution)/shard_map/dot_general | solution.py:82
  252.2 28.3 %all_to_all.92 = bf16[8,144,384]{2,1,0:T(8,128)(2,1)S(1)} all-to-all(bf16[8,144,384]{2,1,0:T(8,128)(2,1)S(1)} %bitcast.270), channel_id=1, replica_groups=mesh['dp'=2,'x'=4,'y'=4,'core'=2,'mlp'=4] {'core','mlp'}, dimensions={0} | all-to-all | bytes 1769472 | tf_op jit(solution)/shard_map/all_to_all | solution.py:86
  282.8 26.0 %all_to_all.93 = bf16[16,72,384]{2,1,0:T(8,128)(2,1)S(1)} all-to-all(bf16[16,72,384]{2,1,0:T(8,128)(2,1)S(1)} %bitcast.272), channel_id=1, replica_groups=mesh['dp'=2,'x'=4,'y'=4,'core'=2,'mlp'=4] {'x','y'}, dimensions={0} | all-to-all | bytes 1769472 | tf_op jit(solution)/shard_map/all_to_all | solution.py:86
  332.3 4.7 fusion.138
  342.2 5.4 %all-to-all-start.12 = ((bf16[16,72,128]{2,1,0:T(8,128)(2,1)}), bf16[16,72,128]{2,1,0:T(8,128)(2,1)S(1)}, u32[]{:S(2)}, u32[]{:S(2)}) async-start(bf16[16,72,128]{2,1,0:T(8,128)(2,1)} %convert_element_type.297), calls=%async_computation.12 | async-start | bytes 589824 | tf_op jit(solution)/shard_map/all_to_all | solution.py:86
  366.4 4.4 all-to-all-start.8
  372.8 9.0 %all-to-all-done.8 = bf16[16,72,384]{2,1,0:T(8,128)(2,1)S(1)} async-done(((bf16[16,72,384]{2,1,0:T(8,128)(2,1)}), bf16[16,72,384]{2,1,0:T(8,128)(2,1)S(1)}, u32[]{:S(2)}, u32[]{:S(2)}) %all-to-all-start.8) | async-done | bytes 884768 | tf_op jit(solution)/shard_map/all_to_all | solution.py:86
  381.8 5.7 %all-to-all-start.17 = ((bf16[8,48,768]{2,1,0:T(8,128)(2,1)}), bf16[8,48,768]{2,1,0:T(8,128)(2,1)}, u32[]{:S(2)}, u32[]{:S(2)}) async-start(bf16[8,48,768]{2,1,0:T(8,128)(2,1)} %pad_maximum_fusion.10), calls=%async_computation.18 | async-start | bytes 1179648 | tf_op jit(solution)/shard_map/all_to_all | solution.py:86
  392.1 10.9 %all-to-all-done.17 = bf16[8,48,768]{2,1,0:T(8,128)(2,1)} async-done(((bf16[8,48,768]{2,1,0:T(8,128)(2,1)}), bf16[8,48,768]{2,1,0:T(8,128)(2,1)}, u32[]{:S(2)}, u32[]{:S(2)}) %all-to-all-start.17) | async-done | bytes 589856 | tf_op jit(solution)/shard_map/all_to_all | solution.py:86
  402.9 6.0 %all-to-all-start.9 = ((bf16[8,144,384]{2,1,0:T(8,128)(2,1)}), bf16[8,144,384]{2,1,0:T(8,128)(2,1)}, u32[]{:S(2)}, u32[]{:S(2)}) async-start(bf16[8,144,384]{2,1,0:T(8,128)(2,1)} %bitcast.52), calls=%async_computation.9 | async-start | bytes 1769472 | tf_op jit(solution)/shard_map/all_to_all | solution.py:86
  418.9 9.3 %all-to-all-done.9 = bf16[8,144,384]{2,1,0:T(8,128)(2,1)} async-done(((bf16[8,144,384]{2,1,0:T(8,128)(2,1)}), bf16[8,144,384]{2,1,0:T(8,128)(2,1)}, u32[]{:S(2)}, u32[]{:S(2)}) %all-to-all-start.9) | async-done | bytes 884768 | tf_op jit(solution)/shard_map/all_to_all | solution.py:86
  429.7 5.5 %all-to-all-start.14 = ((bf16[32,72,128]{2,1,0:T(8,128)(2,1)}), bf16[32,72,128]{2,1,0:T(8,128)(2,1)}, u32[]{:S(2)}, u32[]{:S(2)}) async-start(bf16[32,72,128]{2,1,0:T(8,128)(2,1)} %broadcast_in_dim.56), calls=%async_computation.14 | async-start | bytes 1179648 | tf_op jit(solution)/shard_map/all_to_all | solution.py:86
  439.8 7.8 %all-to-all-done.14 = bf16[32,72,128]{2,1,0:T(8,128)(2,1)} async-done(((bf16[32,72,128]{2,1,0:T(8,128)(2,1)}), bf16[32,72,128]{2,1,0:T(8,128)(2,1)}, u32[]{:S(2)}, u32[]{:S(2)}) %all-to-all-start.14) | async-done | bytes 589856 | tf_op jit(solution)/shard_map/all_to_all | solution.py:86
  448.4 9.7 %all-to-all-start.10 = ((f32[16,36,128]{2,1,0:T(8,128)}), f32[16,36,128]{2,1,0:T(8,128)}, u32[]{:S(2)}, u32[]{:S(2)}) async-start(f32[16,36,128]{2,1,0:T(8,128)} %broadcast_in_dim.53), calls=%async_computation.10 | async-start | bytes 655360 | tf_op jit(solution)/shard_map/all_to_all | solution.py:86
  471.9 5.0 all-to-all-start.15
  481.1 10.2 %all-to-all-done.15 = f32[16,42,128]{2,1,0:T(8,128)} async-done(((f32[16,42,128]{2,1,0:T(8,128)}), f32[16,42,128]{2,1,0:T(8,128)}, u32[]{:S(2)}, u32[]{:S(2)}) %all-to-all-start.15) | async-done | bytes 344096 | tf_op jit(solution)/shard_map/all_to_all | solution.py:86
  492.8 4.4 all-to-all-start.11
  513.5 5.7 %all-to-all-done.16 = f32[16,42,128]{2,1,0:T(8,128)S(1)} async-done(((f32[16,42,128]{2,1,0:T(8,128)}), f32[16,42,128]{2,1,0:T(8,128)S(1)}, u32[]{:S(2)}, u32[]{:S(2)}) %all-to-all-start.16) | async-done | bytes 344096 | tf_op jit(solution)/shard_map/all_to_all | solution.py:86
  (410 shorter events, 204.1 us)
Async XLA Ops:
  7.2 185.4 %all-gather.5.cloned.1.call-start = ((), (), s32[]{:S(2)}) async-start(), calls=%async_computation.20 | async-start | bytes 9732096 | tf_op jit(solution)/shard_map/all_gather | solution.py:171
  10.3 31.8 %copy-start.94 = (f32[2,2,96]{2,1,0:T(2,128)S(1)}, f32[2,2,96]{2,1,0:T(2,128)}, u32[]{:S(2)}) copy-start(f32[2,2,96]{2,1,0:T(2,128)} %param.26) | copy-start | bytes 4612
  10.4 31.9 %copy-start.95 = (f32[2,2,96]{2,1,0:T(2,128)S(1)}, f32[2,2,96]{2,1,0:T(2,128)}, u32[]{:S(2)}) copy-start(f32[2,2,96]{2,1,0:T(2,128)} %param.24) | copy-start | bytes 4612
  10.4 32.0 %copy-start.88 = (f32[768]{0:T(1024)S(1)}, f32[768]{0:T(1024)}, u32[]{:S(2)}) copy-start(f32[768]{0:T(1024)} %param.30) | copy-start | bytes 9220
  10.4 37.2 %copy-start.83 = (s32[4,3,45]{2,0,1:T(4,128)S(1)}, s32[4,3,45]{2,0,1:T(4,128)}, u32[]{:S(2)}) copy-start(s32[4,3,45]{2,0,1:T(4,128)} %param.20) | copy-start | bytes 6484
  10.4 37.2 %copy-start.39 = (bf16[4,3,45,768]{3,0,2,1:T(4,128)(2,1)S(1)}, bf16[4,3,45,768]{3,0,2,1:T(4,128)(2,1)}, u32[]{:S(2)}) copy-start(bf16[4,3,45,768]{3,0,2,1:T(4,128)(2,1)} %param.19) | copy-start | bytes 2488324
  43.0 11.5 %all-to-all-start.3 = ((f32[4,12,128]{2,1,0:T(8,128)}), f32[4,12,128]{2,1,0:T(8,128)}, u32[]{:S(2)}, u32[]{:S(2)}) async-start(f32[4,12,128]{2,1,0:T(8,128)} %broadcast_in_dim.40), calls=%async_computation.3 | async-start | bytes 65536 | tf_op jit(solution)/shard_map/all_to_all | solution.py:86
  47.6 140.4 %copy-start.56 = (f32[4,3,48]{2,1,0:T(4,128)}, f32[4,3,48]{2,1,0:T(4,128)S(1)}, u32[]{:S(2)}) copy-start(f32[4,3,48]{2,1,0:T(4,128)S(1)} %copy.187) | copy-start | bytes 6916
  47.7 140.2 %copy-start = (bf16[4,3,45,768]{3,2,1,0:T(8,128)(2,1)}, bf16[4,3,45,768]{3,2,1,0:T(8,128)(2,1)S(1)}, u32[]{:S(2)}) copy-start(bf16[4,3,45,768]{3,2,1,0:T(8,128)(2,1)S(1)} %copy.186) | copy-start | bytes 2488324
  47.9 140.0 %copy-start.58 = (f32[4,3,48]{2,1,0:T(4,128)}, f32[4,3,48]{2,1,0:T(4,128)S(1)}, u32[]{:S(2)}) copy-start(f32[4,3,48]{2,1,0:T(4,128)S(1)} %broadcast_multiply_fusion.5) | copy-start | bytes 6916
  50.0 35.2 %copy-start.9 = (bf16[1152,1152]{1,0:T(8,128)(2,1)S(1)}, bf16[1152,1152]{1,0:T(8,128)(2,1)}, u32[]{:S(2)}) copy-start(bf16[1152,1152]{1,0:T(8,128)(2,1)} %constant.127.clone) | copy-start | bytes 7962628
  54.4 30.8 %all-to-all-start = ((bf16[8,144,384]{2,1,0:T(8,128)(2,1)}), bf16[8,144,384]{2,1,0:T(8,128)(2,1)}, u32[]{:S(2)}, u32[]{:S(2)}) async-start(bf16[8,144,384]{2,1,0:T(8,128)(2,1)} %bitcast.4), calls=%async_computation | async-start | bytes 1769472 | tf_op jit(solution)/shard_map/all_to_all | solution.py:86
  91.1 21.4 %all-to-all-start.1 = ((bf16[16,72,384]{2,1,0:T(8,128)(2,1)}), bf16[16,72,384]{2,1,0:T(8,128)(2,1)}, u32[]{:S(2)}, u32[]{:S(2)}) async-start(bf16[16,72,384]{2,1,0:T(8,128)(2,1)} %bitcast.7), calls=%async_computation.1 | async-start | bytes 1769472 | tf_op jit(solution)/shard_map/all_to_all | solution.py:86
  101.7 24.8 %copy-start.28 = (bf16[384,384]{1,0:T(8,128)(2,1)}, bf16[384,384]{1,0:T(8,128)(2,1)S(1)}, u32[]{:S(2)}) copy-start(bf16[384,384]{1,0:T(8,128)(2,1)S(1)} %squeeze.69) | copy-start | bytes 884740
  101.8 24.8 %copy-start.49 = (bf16[384,384]{1,0:T(8,128)(2,1)}, bf16[384,384]{1,0:T(8,128)(2,1)S(1)}, u32[]{:S(2)}) copy-start(bf16[384,384]{1,0:T(8,128)(2,1)S(1)} %neg.48) | copy-start | bytes 884740
  153.8 34.1 %all-to-all-start.5 = ((bf16[8,144,384]{2,1,0:T(8,128)(2,1)}), bf16[8,144,384]{2,1,0:T(8,128)(2,1)S(1)}, u32[]{:S(2)}, u32[]{:S(2)}) async-start(bf16[8,144,384]{2,1,0:T(8,128)(2,1)} %bitcast.25), calls=%async_computation.5 | async-start | bytes 1769472 | tf_op jit(solution)/shard_map/all_to_all | solution.py:86
  164.3 206.6 %reduce-scatter.2.cloned.1.call-start = ((), (), s32[]{:S(2)}) async-start(), calls=%async_computation.19 | async-start | bytes 9732096 | tf_op jit(solution)/shard_map/reduce_scatter | solution.py:255
  164.4 26.4 %copy-start.2 = (bf16[4,3,45,768]{3,2,1,0:T(8,128)(2,1)}, bf16[4,3,45,768]{3,2,1,0:T(8,128)(2,1)S(1)}, u32[]{:S(2)}) copy-start(bf16[4,3,45,768]{3,2,1,0:T(8,128)(2,1)S(1)} %copy.195) | copy-start | bytes 2488324
  196.9 20.6 %copy-start.14 = (bf16[16,1,48,768]{3,2,1,0:T(8,128)(2,1)}, bf16[16,1,48,768]{3,2,1,0:T(8,128)(2,1)S(1)}, u32[]{:S(2)}) copy-start(bf16[16,1,48,768]{3,2,1,0:T(8,128)(2,1)S(1)} %get-tuple-element.128) | copy-start | bytes 3538948
  203.2 21.1 %copy-start.103 = (bf16[576,768]{1,0:T(8,128)(2,1)}, bf16[576,768]{1,0:T(8,128)(2,1)S(1)}, u32[]{:S(2)}) copy-start(bf16[576,768]{1,0:T(8,128)(2,1)S(1)} %get-tuple-element.100) | copy-start | bytes 2654212
  252.1 28.4 %copy-start.10 = (bf16[1152,1152]{1,0:T(8,128)(2,1)S(1)}, bf16[1152,1152]{1,0:T(8,128)(2,1)}, u32[]{:S(2)}) copy-start(bf16[1152,1152]{1,0:T(8,128)(2,1)} %constant.128.clone) | copy-start | bytes 7962628
  342.2 12.9 %all-to-all-start.12 = ((bf16[16,72,128]{2,1,0:T(8,128)(2,1)}), bf16[16,72,128]{2,1,0:T(8,128)(2,1)S(1)}, u32[]{:S(2)}, u32[]{:S(2)}) async-start(bf16[16,72,128]{2,1,0:T(8,128)(2,1)} %convert_element_type.297), calls=%async_computation.12 | async-start | bytes 589824 | tf_op jit(solution)/shard_map/all_to_all | solution.py:86
  355.8 10.6 %all-to-all-start.13 = ((bf16[8,72,128]{2,1,0:T(8,128)(2,1)}), bf16[8,72,128]{2,1,0:T(8,128)(2,1)S(1)}, u32[]{:S(2)}, u32[]{:S(2)}) async-start(bf16[8,72,128]{2,1,0:T(8,128)(2,1)} %broadcast_in_dim.55), calls=%async_computation.13 | async-start | bytes 294912 | tf_op jit(solution)/shard_map/all_to_all | solution.py:86
  366.4 15.4 %all-to-all-start.8 = ((bf16[16,72,384]{2,1,0:T(8,128)(2,1)}), bf16[16,72,384]{2,1,0:T(8,128)(2,1)S(1)}, u32[]{:S(2)}, u32[]{:S(2)}) async-start(bf16[16,72,384]{2,1,0:T(8,128)(2,1)} %bitcast.49), calls=%async_computation.8 | async-start | bytes 1769472 | tf_op jit(solution)/shard_map/all_to_all | solution.py:86
  381.8 21.1 %all-to-all-start.17 = ((bf16[8,48,768]{2,1,0:T(8,128)(2,1)}), bf16[8,48,768]{2,1,0:T(8,128)(2,1)}, u32[]{:S(2)}, u32[]{:S(2)}) async-start(bf16[8,48,768]{2,1,0:T(8,128)(2,1)} %pad_maximum_fusion.10), calls=%async_computation.18 | async-start | bytes 1179648 | tf_op jit(solution)/shard_map/all_to_all | solution.py:86
  402.9 25.2 %all-to-all-start.9 = ((bf16[8,144,384]{2,1,0:T(8,128)(2,1)}), bf16[8,144,384]{2,1,0:T(8,128)(2,1)}, u32[]{:S(2)}, u32[]{:S(2)}) async-start(bf16[8,144,384]{2,1,0:T(8,128)(2,1)} %bitcast.52), calls=%async_computation.9 | async-start | bytes 1769472 | tf_op jit(solution)/shard_map/all_to_all | solution.py:86
  408.9 112.9 %all-gather.7.cloned.1.call-start = ((), (), s32[]{:S(2)}) async-start(), calls=%async_computation.21 | async-start | bytes 2433024 | tf_op jit(solution)/shard_map/all_gather | solution.py:259
  429.7 17.9 %all-to-all-start.14 = ((bf16[32,72,128]{2,1,0:T(8,128)(2,1)}), bf16[32,72,128]{2,1,0:T(8,128)(2,1)}, u32[]{:S(2)}, u32[]{:S(2)}) async-start(bf16[32,72,128]{2,1,0:T(8,128)(2,1)} %broadcast_in_dim.56), calls=%async_computation.14 | async-start | bytes 1179648 | tf_op jit(solution)/shard_map/all_to_all | solution.py:86
  448.4 22.8 %all-to-all-start.10 = ((f32[16,36,128]{2,1,0:T(8,128)}), f32[16,36,128]{2,1,0:T(8,128)}, u32[]{:S(2)}, u32[]{:S(2)}) async-start(f32[16,36,128]{2,1,0:T(8,128)} %broadcast_in_dim.53), calls=%async_computation.10 | async-start | bytes 655360 | tf_op jit(solution)/shard_map/all_to_all | solution.py:86
  471.9 19.4 %all-to-all-start.15 = ((f32[16,42,128]{2,1,0:T(8,128)}), f32[16,42,128]{2,1,0:T(8,128)}, u32[]{:S(2)}, u32[]{:S(2)}) async-start(f32[16,42,128]{2,1,0:T(8,128)} %broadcast_in_dim.57), calls=%async_computation.15 | async-start | bytes 786432 | tf_op jit(solution)/shard_map/all_to_all | solution.py:86
  492.8 12.3 %all-to-all-start.11 = ((f32[16,36,128]{2,1,0:T(8,128)}), f32[16,36,128]{2,1,0:T(8,128)}, u32[]{:S(2)}, u32[]{:S(2)}) async-start(f32[16,36,128]{2,1,0:T(8,128)} %broadcast_in_dim.54), calls=%async_computation.11 | async-start | bytes 655360 | tf_op jit(solution)/shard_map/all_to_all | solution.py:86
  505.9 13.4 %all-to-all-start.16 = ((f32[16,42,128]{2,1,0:T(8,128)}), f32[16,42,128]{2,1,0:T(8,128)S(1)}, u32[]{:S(2)}, u32[]{:S(2)}) async-start(f32[16,42,128]{2,1,0:T(8,128)} %broadcast_in_dim.58), calls=%async_computation.16 | async-start | bytes 786432 | tf_op jit(solution)/shard_map/all_to_all | solution.py:86
  (94 other events, 574.6 us)
Sparse Core Ops, SparseCore 0:
  42.3 60.8 all-gather.4
  237.3 100.8 reduce-scatter.1
  412.6 50.2 all-gather.6

commit v2 on v1

v2 whole, which is shorter than its diff:
```python
import math

import jax
import jax.numpy as jnp
import numpy as np
from jax import lax
from jax.experimental import pallas as pl
from jax.experimental.pallas import tpu as pltpu
from jax.sharding import Mesh
from jax.sharding import PartitionSpec as P

H = 96
KWP = 96
W = 180
LON = 45
PAD = 48
EPSILON = 1e-05
SHRINK = 0.01
ROOT_HALF = math.sqrt(0.5)
ROOT_TWO_PI = math.sqrt(2.0 * math.pi)

XY = ("x", "y")
PAIR = ("core", "mlp")
EVERY = ("dp", "x", "y", "core", "mlp")
bf16 = jnp.bfloat16
f32 = jnp.float32
ROOM = pltpu.CompilerParams(vmem_limit_bytes=50 * 1024 * 1024)


def tables():
    w = np.arange(W)
    k = np.arange(KWP)
    phase = 2.0 * np.pi * ((w[:, None] * k[None, :]) % W) / W
    live = np.where(k < W // 2 + 1, 1.0 / math.sqrt(W), 0.0)
    weight = np.where((k == 0) | (2 * k == W), 1.0, 2.0) * live
    fwd = np.stack([np.cos(phase) * live, -np.sin(phase) * live], axis=2)
    inv = np.stack([np.cos(phase) * weight, -np.sin(phase) * weight], axis=2)
    pad = ((0, 0), (0, PAD - LON), (0, 0), (0, 0))
    fwd = np.pad(fwd.reshape(4, LON, KWP, 2), pad).reshape(4, PAD, 16, 6, 2)
    inv = np.pad(inv.reshape(4, LON, KWP, 2), pad).reshape(4, PAD, 16, 6, 2)
    same = np.eye(6).reshape(2, 3, 6)
    lon_fwd = np.einsum("mwqkp,rih->qhkprmiw", fwd, same).reshape(1152, 1152)
    lon_inv = np.einsum("mwqkp,rih->rmiwqhkp", inv, same).reshape(1152, 1152)
    h = np.arange(H)
    angle = 2.0 * np.pi * ((h[:, None] * h[None, :]) % H) / H
    cos = np.cos(angle) / math.sqrt(H)
    sin = np.sin(angle) / math.sqrt(H)
    lat_fwd = np.stack([np.stack([cos, sin]), np.stack([-sin, cos])])
    lat_inv = np.stack([np.stack([cos, -sin]), np.stack([sin, cos])])
    kk = np.eye(6).reshape(2, 3, 6)
    grid_fwd = np.einsum("pqjah,tkl->tpkjahlq", lat_fwd.reshape(2, 2, H, 16, 6), kk)
    grid_inv = np.einsum("pqahj,tkl->tahlpqkj", lat_inv.reshape(2, 2, 16, 6, H), kk)
    grid_fwd = grid_fwd.reshape(2, 576, 1152)
    grid_inv = grid_inv.reshape(2, 1152, 576)

    def low(table):
        return np.ascontiguousarray(table).astype(np.float32).astype(bf16)

    return {
        "lon_fwd": low(lon_fwd),
        "lon_inv": low(lon_inv),
        "lon_fwd_t": low(lon_fwd.T),
        "lon_inv_t": low(lon_inv.T),
        "grid_fwd": low(grid_fwd),
        "grid_inv": low(grid_inv),
        "grid_fwd_t": low(grid_fwd.swapaxes(1, 2)),
        "grid_inv_t": low(grid_inv.swapaxes(1, 2)),
    }


def block_fold():
    at = np.arange(384) // 96
    mask = (at[:, None] == at[None, :]).astype(np.float32)
    fold = np.tile(np.eye(96, 128), (4, 1))
    return mask, fold.astype(np.float32).astype(bf16)


def mm(left, right):
    return jnp.dot(left, right, preferred_element_type=f32)


def inner_rows(left, right):
    return lax.dot_general(left, right, (((0,), (0,)), ((), ())), preferred_element_type=f32)


def outer_cols(left, right):
    return lax.dot_general(left, right, (((1,), (1,)), ((), ())), preferred_element_type=f32)


def gelu_parts(value):
    half = 0.5 * (1.0 + lax.erf(value * ROOT_HALF))
    return half, jnp.exp(-0.5 * value * value) * (1.0 / ROOT_TWO_PI)


def standard(value):
    centred = value - jnp.mean(value, axis=-1, keepdims=True)
    scale = lax.rsqrt(jnp.mean(centred * centred, axis=-1, keepdims=True) + EPSILON)
    return centred * scale, scale


def widen(rows, source):
    for i in range(3):
        rows[PAD * i : PAD * i + LON, :] = source[i].astype(f32)
    return rows[...]


def both_halves(pair, s):
    return jnp.concatenate([pair[0, s], pair[1, s]], axis=-1).astype(f32)


def whole(shape):
    return pl.BlockSpec(shape, lambda *_: (0,) * len(shape))


def struct(shape, dtype):
    return jax.ShapeDtypeStruct(shape, dtype)


def norm_kernel(x, present, gain, shift, out, rows):
    rows[...] = jnp.zeros_like(rows)
    normed, _ = standard(widen(rows, x.at[0]))
    masked = ((normed * gain[...] + shift[...]) * present[...]).astype(bf16)
    out[0, 0] = masked[:, :384]
    out[1, 0] = masked[:, 384:]


def norm_pack(inputs, present, gain, shift):
    return pl.pallas_call(
        norm_kernel,
        grid=(4,),
        in_specs=[
            pl.BlockSpec((1, 3, LON, 768), lambda s: (s, 0, 0, 0)),
            pl.BlockSpec((144, 1), lambda s: (s, 0)),
            whole((1, 768)),
            whole((1, 768)),
        ],
        out_specs=pl.BlockSpec((2, 1, 144, 384), lambda s: (0, s, 0, 0)),
        out_shape=struct((2, 4, 144, 384), bf16),
        scratch_shapes=[pltpu.VMEM((144, 768), f32)],
        compiler_params=ROOM,
    )(inputs, present, gain, shift)


def table_kernel(table, rows, out):
    out[...] = mm(table[...], rows[...]).astype(bf16)


def transform(table, rows):
    return pl.pallas_call(
        table_kernel,
        grid=(3,),
        in_specs=[pl.BlockSpec((384, 1152), lambda t: (t, 0)), whole((1152, 384))],
        out_specs=pl.BlockSpec((384, 384), lambda t: (t, 0)),
        out_shape=struct((1152, 384), bf16),
        compiler_params=ROOM,
    )(table, rows)


def filter_kernel(
    rows, fwd, inv, mix_in, mix_out, bias_in, bias_out, back, low, first, active, second, total
):
    grid = mm(fwd[0], rows[...]).astype(bf16)
    grid = jnp.concatenate([grid[:288], grid[288:]], axis=1)
    low[...] = grid
    value = mm(grid, mix_in[...]) + bias_in[...]
    first[...] = value
    half, _ = gelu_parts(value)
    hot = (value * half).astype(bf16)
    active[...] = hot
    value = mm(hot, mix_out[...]) + bias_out[...]
    second[...] = value
    value = value - SHRINK * value * lax.rsqrt(value * value + SHRINK * SHRINK)
    value = value.astype(bf16)
    value = jnp.concatenate([value[:, :384], value[:, 384:]], axis=0)
    part = mm(inv[0], value)

    @pl.when(pl.program_id(0) == 0)
    def _():
        total[...] = part

    @pl.when(pl.program_id(0) == 1)
    def _():
        back[...] = (total[...] + part).astype(bf16)


def filter_forward(rows, fwd, inv, mix_in, mix_out, bias_in, bias_out):
    part = pl.BlockSpec((288, 768), lambda t: (t, 0))
    return pl.pallas_call(
        filter_kernel,
        grid=(2,),
        in_specs=[
            whole((1152, 384)),
            pl.BlockSpec((1, 576, 1152), lambda t: (t, 0, 0)),
            pl.BlockSpec((1, 1152, 576), lambda t: (t, 0, 0)),
            whole((768, 768)),
            whole((768, 768)),
            whole((1, 768)),
            whole((1, 768)),
        ],
        out_specs=[whole((1152, 384)), part, part, part, part],
        out_shape=[
            struct((1152, 384), bf16),
            struct((576, 768), bf16),
            struct((576, 768), f32),
            struct((576, 768), bf16),
            struct((576, 768), f32),
        ],
        scratch_shapes=[pltpu.VMEM((1152, 384), f32)],
        compiler_params=ROOM,
    )(rows, fwd, inv, mix_in, mix_out, bias_in, bias_out)


def filter_back_kernel(
    rows, inv_t, fwd_t, mix_in, mix_out, first, second, back, first_low, second_low, sums, total
):
    step = pl.program_id(0)
    grad = mm(inv_t[0], rows[...])
    grad = jnp.concatenate([grad[:288], grad[288:]], axis=1)
    value = second[...]
    root = lax.rsqrt(value * value + SHRINK * SHRINK)
    grad = grad * (1.0 - SHRINK * SHRINK * SHRINK * root * root * root)
    out_sum = jnp.sum(grad, axis=0, keepdims=True)
    grad = grad.astype(bf16)
    second_low[...] = grad
    value = first[...]
    half, bell = gelu_parts(value)
    grad = outer_cols(grad, mix_out[...]) * (half + value * bell)
    in_sum = jnp.sum(grad, axis=0, keepdims=True)
    grad = grad.astype(bf16)
    first_low[...] = grad
    grad = outer_cols(grad, mix_in[...]).astype(bf16)
    grad = jnp.concatenate([grad[:, :384], grad[:, 384:]], axis=0)
    part = mm(fwd_t[0], grad)

    @pl.when(step == 0)
    def _():
        total[...] = part
        sums[0:1, :] = in_sum
        sums[1:2, :] = out_sum

    @pl.when(step == 1)
    def _():
        back[...] = (total[...] + part).astype(bf16)
        sums[0:1, :] += in_sum
        sums[1:2, :] += out_sum


def filter_backward(rows, inv_t, fwd_t, mix_in, mix_out, first, second):
    part = pl.BlockSpec((288, 768), lambda t: (t, 0))
    return pl.pallas_call(
        filter_back_kernel,
        grid=(2,),
        in_specs=[
            whole((1152, 384)),
            pl.BlockSpec((1, 576, 1152), lambda t: (t, 0, 0)),
            pl.BlockSpec((1, 1152, 576), lambda t: (t, 0, 0)),
            whole((768, 768)),
            whole((768, 768)),
            part,
            part,
        ],
        out_specs=[whole((1152, 384)), part, part, whole((2, 768))],
        out_shape=[
            struct((1152, 384), bf16),
            struct((576, 768), bf16),
            struct((576, 768), bf16),
            struct((2, 768), f32),
        ],
        scratch_shapes=[pltpu.VMEM((1152, 384), f32)],
        compiler_params=ROOM,
    )(rows, inv_t, fwd_t, mix_in, mix_out, first, second)


def filter_grads_kernel(low, first_low, active, second_low, mask, fold, out):
    for which, (left, right) in enumerate(((low, first_low), (active, second_low))):
        grad = inner_rows(left[...], right[...])
        real = grad[:384, :384] + grad[384:, 384:]
        imag = grad[:384, 384:] - grad[384:, :384]
        for part, value in enumerate((real, imag)):
            blocks = mm((value * mask[...]).astype(bf16), fold[...]).astype(bf16)
            for piece in range(3):
                at = which * 768 + part * 384 + piece * 128
                group, row = at // 256, at % 256
                out[row : row + 128, group * 128 : group * 128 + 128] = blocks[
                    piece * 128 : piece * 128 + 128
                ]


def filter_grads(low, first_low, active, second_low, mask, fold):
    return pl.pallas_call(
        filter_grads_kernel,
        out_shape=struct((256, 768), bf16),
        compiler_params=ROOM,
    )(low, first_low, active, second_low, mask, fold)


def chain_kernel(
    x, present, filtered, cotangent, gain_first, shift_first, gain, shift, w_in, w_out, units,
    stream, mixed, grad_low, hidden, grad_pre, grad_stream, packed, sums, unit_sums,
    rows, normed, scale, total,
):
    step = pl.program_id(0)

    @pl.when(step == 0)
    def _():
        rows[...] = jnp.zeros_like(rows)
        total[...] = jnp.zeros_like(total)
        sums[...] = jnp.zeros_like(sums)
        for s in range(4):
            here = slice(144 * s, 144 * s + 144)
            there = present[here]
            value = widen(rows, x.at[s])
            first, _ = standard(value)
            masked = (first * gain_first[...] + shift_first[...]) * there
            value = value + both_halves(filtered, s) + masked
            stream[here] = value
            value, spread_of = standard(value.astype(bf16).astype(f32))
            normed[here] = value
            scale[here] = spread_of
            mixed[here] = (value * gain[...] + shift[...]).astype(bf16)
            value = widen(rows, cotangent.at[s]) * there
            sums[2:3, :] += jnp.sum(value, axis=0, keepdims=True)
            grad_low[here] = value.astype(bf16)

    into = w_in[...].reshape(768, 768)
    outof = w_out[...].reshape(768, 768)
    unit_total = jnp.zeros((1, 768), f32)
    for b in range(2):
        here = slice(288 * b, 288 * b + 288)
        value = mm(mixed[here], into) + units[0]
        half, bell = gelu_parts(value)
        hidden[0, here] = (value * half).astype(bf16)
        grad = outer_cols(grad_low[here], outof) * (half + value * bell)
        unit_total += jnp.sum(grad, axis=0, keepdims=True)
        grad = grad.astype(bf16)
        grad_pre[0, here] = grad
        total[here] += outer_cols(grad, into).astype(bf16).astype(f32)
    unit_sums[0] = unit_total

    @pl.when(step == 3)
    def _():
        for s in range(4):
            here = slice(144 * s, 144 * s + 144)
            grad = total[here]
            value = normed[here]
            sums[0:1, :] += jnp.sum(grad * value, axis=0, keepdims=True)
            sums[1:2, :] += jnp.sum(grad, axis=0, keepdims=True)
            grad = grad * gain[...]
            grad = grad - jnp.mean(grad, axis=-1, keepdims=True) - value * jnp.mean(
                grad * value, axis=-1, keepdims=True
            )
            grad = widen(rows, cotangent.at[s]) + scale[here] * grad
            grad_stream[here] = grad
            packed[0, s] = grad[:, :384].astype(bf16)
            packed[1, s] = grad[:, 384:].astype(bf16)


def chain(x, present, filtered, cotangent, gain_first, shift_first, gain, shift, weights, units):
    group = pl.BlockSpec((1, 576, 768), lambda g: (g, 0, 0))
    return pl.pallas_call(
        chain_kernel,
        grid=(4,),
        in_specs=[
            whole((4, 3, LON, 768)),
            whole((576, 1)),
            whole((2, 4, 144, 384)),
            whole((4, 3, LON, 768)),
            whole((1, 768)),
            whole((1, 768)),
            whole((1, 768)),
            whole((1, 768)),
            pl.BlockSpec((16, 1, PAD, 768), lambda g: (0, g, 0, 0)),
            pl.BlockSpec((16, 1, PAD, 768), lambda g: (1, g, 0, 0)),
            pl.BlockSpec((1, 1, 768), lambda g: (g, 0, 0)),
        ],
        out_specs=[
            whole((576, 768)),
            whole((576, 768)),
            whole((576, 768)),
            group,
            group,
            whole((576, 768)),
            whole((2, 4, 144, 384)),
            whole((3, 768)),
            pl.BlockSpec((1, 1, 768), lambda g: (g, 0, 0)),
        ],
        out_shape=[
            struct((576, 768), f32),
            struct((576, 768), bf16),
            struct((576, 768), bf16),
            struct((4, 576, 768), bf16),
            struct((4, 576, 768), bf16),
            struct((576, 768), f32),
            struct((2, 4, 144, 384), bf16),
            struct((3, 768), f32),
            struct((4, 1, 768), f32),
        ],
        scratch_shapes=[
            pltpu.VMEM((144, 768), f32),
            pltpu.VMEM((576, 768), f32),
            pltpu.VMEM((576, 1), f32),
            pltpu.VMEM((576, 768), f32),
        ],
        compiler_params=ROOM,
    )(x, present, filtered, cotangent, gain_first, shift_first, gain, shift, weights, weights, units)


def weight_grads_kernel(core, mixed, grad_pre, hidden, grad_low, out):
    @pl.when(pl.program_id(1) == 0)
    def _():
        out[...] = inner_rows(mixed[...], grad_pre[0]).astype(bf16).reshape(1, 16, 1, PAD, 768)

    @pl.when(pl.program_id(1) == 1)
    def _():
        out[...] = inner_rows(hidden[0], grad_low[...]).astype(bf16).reshape(1, 16, 1, PAD, 768)


def weight_grads(core, mixed, grad_pre, hidden, grad_low):
    group = pl.BlockSpec((1, 576, 768), lambda g, w, c: (g, 0, 0))
    return pl.pallas_call(
        weight_grads_kernel,
        grid_spec=pltpu.PrefetchScalarGridSpec(
            num_scalar_prefetch=1,
            grid=(4, 2),
            in_specs=[whole((576, 768)), group, group, whole((576, 768))],
            out_specs=pl.BlockSpec(
                (1, 16, 1, PAD, 768), lambda g, w, c: ((w + c[0]) % 2, 0, g, 0, 0)
            ),
        ),
        out_shape=struct((2, 16, 4, PAD, 768), bf16),
        compiler_params=ROOM,
    )(core, mixed, grad_pre, hidden, grad_low)


def output_kernel(hidden, w_out, stream, present, bias, out, total):
    step = pl.program_id(0)
    part = mm(hidden[0], w_out[...].reshape(768, 768)).astype(bf16).astype(f32)

    @pl.when(step == 0)
    def _():
        total[...] = part

    @pl.when(step > 0)
    def _():
        total[...] += part

    @pl.when(step == 3)
    def _():
        for s in range(4):
            here = slice(144 * s, 144 * s + 144)
            value = stream[here] + present[here] * (total[here] + bias[...])
            for i in range(3):
                out[s, i] = value[PAD * i : PAD * i + LON].astype(bf16)


def layer_output(hidden, weights, stream, present, bias):
    return pl.pallas_call(
        output_kernel,
        grid=(4,),
        in_specs=[
            pl.BlockSpec((1, 576, 768), lambda g: (g, 0, 0)),
            pl.BlockSpec((16, 1, PAD, 768), lambda g: (1, g, 0, 0)),
            whole((576, 768)),
            whole((576, 1)),
            whole((1, 768)),
        ],
        out_specs=whole((4, 3, LON, 768)),
        out_shape=struct((4, 3, LON, 768), bf16),
        scratch_shapes=[pltpu.VMEM((576, 768), f32)],
        compiler_params=ROOM,
    )(hidden, weights, stream, present, bias)


def final_kernel(x, present, from_spec, grad_stream, gain, out, sums, rows):
    @pl.when(pl.program_id(0) == 0)
    def _():
        sums[...] = jnp.zeros_like(sums)

    rows[...] = jnp.zeros_like(rows)
    normed, scale = standard(widen(rows, x.at[0]))
    stream = grad_stream[...]
    grad = (both_halves(from_spec, 0) + stream) * present[...]
    sums[0:1, :] += jnp.sum(grad * normed, axis=0, keepdims=True)
    sums[1:2, :] += jnp.sum(grad, axis=0, keepdims=True)
    grad = grad * gain[...]
    grad = grad - jnp.mean(grad, axis=-1, keepdims=True) - normed * jnp.mean(
        grad * normed, axis=-1, keepdims=True
    )
    grad = stream + scale * grad
    for i in range(3):
        out[0, i] = grad[PAD * i : PAD * i + LON]


def input_grads(x, present, from_spec, grad_stream, gain):
    return pl.pallas_call(
        final_kernel,
        grid=(4,),
        in_specs=[
            pl.BlockSpec((1, 3, LON, 768), lambda s: (s, 0, 0, 0)),
            pl.BlockSpec((144, 1), lambda s: (s, 0)),
            pl.BlockSpec((2, 1, 144, 384), lambda s: (0, s, 0, 0)),
            pl.BlockSpec((144, 768), lambda s: (s, 0)),
            whole((1, 768)),
        ],
        out_specs=[
            pl.BlockSpec((1, 3, LON, 768), lambda s: (s, 0, 0, 0)),
            whole((2, 768)),
        ],
        out_shape=[struct((4, 3, LON, 768), f32), struct((2, 768), f32)],
        scratch_shapes=[pltpu.VMEM((144, 768), f32)],
        compiler_params=ROOM,
    )(x, present, from_spec, grad_stream, gain)


def swap(value, axes):
    return lax.all_to_all(value, axes, 0, 0, tiled=True)


def spread(value, axes, count):
    return swap(jnp.broadcast_to(value[None], (count,) + value.shape), axes)


def shifted(value, by):
    return lax.ppermute(value, "mlp", [(i, (i + by) % 4) for i in range(4)])


def across(rows):
    return swap(rows.reshape(16, 72, 384), XY).reshape(1152, 384)


def narrow(rows):
    return jnp.concatenate([rows[..., :384], rows[..., 384:]], axis=-2)


def broad(rows):
    n = rows.shape[-2] // 2
    return jnp.concatenate([rows[..., :n, :], rows[..., n:, :]], axis=-1)


def block_form(weights):
    eye = jnp.eye(4, dtype=weights.dtype)
    dense = jnp.einsum("pbef,bc->pbecf", weights, eye).reshape(2, 384, 384)
    return jnp.concatenate(
        [
            jnp.concatenate([dense[0], dense[1]], axis=1),
            jnp.concatenate([-dense[1], dense[0]], axis=1),
        ],
        axis=0,
    )


def total_of(vector):
    near = jnp.sum(spread(vector, ("dp", "core", "mlp"), 16), axis=0)
    return jnp.sum(spread(near, XY, 16), axis=0)


def after(value, *others):
    return lax.optimization_barrier((value,) + others)[0]


def shards(
    inputs,
    validity,
    gain_first,
    shift_first,
    spectral_in,
    spectral_in_bias,
    spectral_out,
    spectral_out_bias,
    gain_second,
    shift_second,
    weight_in,
    bias_in,
    weight_out,
    bias_out,
    cotangent,
):
    core = lax.axis_index("core")
    group = lax.axis_index("mlp")
    table = {name: jnp.asarray(value) for name, value in tables().items()}
    mask, fold = (jnp.asarray(value) for value in block_fold())
    gain_first, shift_first, gain_second, shift_second, bias_out = (
        value.reshape(1, 768)
        for value in (gain_first, shift_first, gain_second, shift_second, bias_out)
    )

    wide = lax.axis_index(("x", "y", "core"))
    both = jnp.concatenate([weight_in, weight_out], axis=0)
    piece = lax.dynamic_slice_in_dim(both, wide * PAD, PAD, 0)
    piece = jnp.stack([piece] + [shifted(piece, d) for d in (1, 2, 3)])
    weights = lax.all_gather(piece, ("x", "y", "core"))

    present = jnp.pad(validity.astype(f32), ((0, 0), (0, 0), (0, PAD - LON))).reshape(576, 1)
    packed = norm_pack(inputs, present, gain_first, shift_first)
    tokens = swap(packed.reshape(8, 144, 384), PAIR)

    small = after(
        jnp.concatenate([bias_in, spectral_in_bias.reshape(-1), spectral_out_bias.reshape(-1)]), tokens
    )
    filters = after(jnp.stack([spectral_in, spectral_out]), tokens)
    small = jnp.stack([small] + [shifted(small, d) for d in (1, 2, 3)])
    filters = jnp.stack([filters] + [shifted(filters, d) for d in (1, 2, 3)])

    def my_half(value):
        pair = [
            lax.dynamic_index_in_dim(value, (group - 2 * core - u) % 4, 0, keepdims=False)
            for u in range(2)
        ]
        return jnp.concatenate(pair, axis=1)

    units = small[:, :768].reshape(4, 1, 768)
    mix_in = block_form(my_half(filters[:, 0]))
    mix_out = block_form(my_half(filters[:, 1]))
    mix_in_bias = my_half(small[:, 768:1152].reshape(4, 2, 2, 96)).reshape(1, 768)
    mix_out_bias = my_half(small[:, 1152:].reshape(4, 2, 2, 96)).reshape(1, 768)

    spectrum = transform(table["lon_fwd"], tokens.reshape(1152, 384))
    back, grid_low, first, active, second = filter_forward(
        across(spectrum),
        table["grid_fwd"],
        table["grid_inv"],
        mix_in,
        mix_out,
        mix_in_bias,
        mix_out_bias,
    )
    filtered = transform(table["lon_inv"], across(back))
    filtered = swap(filtered.reshape(8, 144, 384), PAIR).reshape(2, 4, 144, 384)

    stream, mixed, grad_low, hidden, grad_pre, grad_stream, packed, sums, unit_sums = chain(
        inputs,
        present,
        filtered,
        cotangent,
        gain_first,
        shift_first,
        gain_second,
        shift_second,
        weights,
        units,
    )
    tokens = swap(packed.reshape(8, 144, 384), PAIR)
    slots = weight_grads(core.astype(jnp.int32).reshape(1), mixed, grad_pre, hidden, grad_low)
    taken = lax.ppermute(slots[1], "core", [(0, 1), (1, 0)])
    share = (slots[0].astype(f32) + taken.astype(f32)).astype(bf16).reshape(3072, 768)
    share = lax.psum_scatter(share, "x", scatter_dimension=0, tiled=True)
    share = lax.psum_scatter(share, "y", scatter_dimension=0, tiled=True)
    output = layer_output(hidden, weights, stream, present, bias_out)

    grad_columns = across(transform(table["lon_inv_t"], tokens.reshape(1152, 384)))
    grad_spectrum, first_low, second_low, filter_sums = filter_backward(
        grad_columns, table["grid_inv_t"], table["grid_fwd_t"], mix_in, mix_out, first, second
    )
    filter_share = filter_grads(grid_low, first_low, active, second_low, mask, fold)
    joined = swap(
        jnp.concatenate(
            [grad_spectrum.reshape(16, 72, 384), narrow(filter_share.reshape(16, 16, 768))], axis=1
        ),
        XY,
    )
    grad_rows = joined[:, :72].reshape(1152, 384)
    filter_share = jnp.sum(joined[:, 72:].astype(f32), axis=0).astype(bf16)
    from_spec = transform(table["lon_fwd_t"], grad_rows)

    order = (group - jnp.arange(4, dtype=jnp.int32)) % 4
    share = jnp.take(narrow(share.reshape(4, PAD, 768)), order, axis=0)
    share = jnp.broadcast_to(share[None], (2, 4, 96, 384)).reshape(8, 96, 384)
    joined = swap(
        jnp.concatenate(
            [
                from_spec.reshape(8, 144, 384),
                share,
                jnp.broadcast_to(filter_share[None], (8, 32, 384)),
            ],
            axis=1,
        ),
        PAIR,
    )
    from_spec = joined[:, :144].reshape(2, 4, 144, 384)
    share = jnp.sum(joined[:, 144:].reshape(2, 4, 128, 384).astype(f32), axis=1).astype(bf16)
    other = lax.ppermute(share, "dp", [(0, 1), (1, 0)])
    share = (share.astype(f32) + other.astype(f32)).astype(bf16)
    gathered = lax.all_gather(share, XY)
    grad_slices = broad(gathered[:, :, :96]).swapaxes(0, 1).reshape(2, 768, 768).astype(f32)
    filters = broad(gathered[:, :, 96:]).reshape(16, 2, 16, 6, 128)[..., :96]
    filters = filters.transpose(1, 3, 0, 2, 4).reshape(2, 2, 2, 4, 96, 96)
    filters = filters.transpose(1, 2, 0, 3, 4, 5).reshape(2, 2, 8, 96, 96).astype(f32)

    grad_inputs, first_sums = input_grads(inputs, present, from_spec, grad_stream, gain_first)

    filter_sums = filter_sums.reshape(2, 2, 1, 384)
    filter_sums = jnp.where(
        core == jnp.arange(2, dtype=jnp.int32)[None, None, :, None], filter_sums, 0.0
    )
    unit_sums = jnp.take(unit_sums.reshape(4, 768), order, axis=0)
    small = total_of(
        jnp.concatenate(
            [first_sums, sums, unit_sums, filter_sums.reshape(4, 768), jnp.zeros((3, 768), f32)]
        )
    )
    filter_sums = small[9:13].reshape(2, 2, 8, 96)
    unit_sums = lax.dynamic_index_in_dim(small[5:9], group, 0, keepdims=False)

    def mine(vector):
        return lax.dynamic_slice_in_dim(vector, group * 192, 192, 0)

    return (
        output,
        grad_inputs,
        mine(small[0]),
        mine(small[1]),
        filters[0],
        filter_sums[0],
        filters[1],
        filter_sums[1],
        mine(small[2]),
        mine(small[3]),
        grad_slices[0],
        unit_sums,
        grad_slices[1],
        mine(small[4]),
    )


def solution(mesh):
    fine = Mesh(mesh.devices.reshape(2, 4, 4, 2, 4), EVERY)
    tokens = P("dp", ("x", "y", "core"), "mlp")
    placed = (
        tokens,
        tokens,
        P(),
        P(),
        P(None, "mlp"),
        P(None, "mlp"),
        P(None, "mlp"),
        P(None, "mlp"),
        P(),
        P(),
        P(None, "mlp"),
        P("mlp"),
        P("mlp", None),
        P(),
        tokens,
    )
    return jax.shard_map(
        shards,
        mesh=fine,
        in_specs=placed,
        out_specs=(
            tokens,
            tokens,
            P("mlp"),
            P("mlp"),
            P(),
            P(),
            P(),
            P(),
            P("mlp"),
            P("mlp"),
            P(None, "mlp"),
            P("mlp"),
            P("mlp", None),
            P("mlp"),
        ),
        check_vma=False,
    )
```

time: 540 us -> 469 us (0.87)
  matrix products: 98 us -> 0 us
  Pallas kernels: 0 us -> 83.9 us
  local copies, waits for them, and re-layouts: 89.1 us -> 42.4 us
  blocking collectives: 102 us -> 128 us
  starting transfers between devices: 84 us -> 66.6 us
  other arithmetic: 35.4 us -> 18.6 us
    dot_general x40 -> x0, matrix products: 98 us -> none  [the longest x15 36.1 us: mm(): return jnp.dot(left, right, preferred_element_type=f32)]
    pallas_call x0 -> x12, Pallas kernels: none -> 83.9 us  [the longest x1 17.7 us: chain(): pl.pallas_call(chain_kernel, grid=(4,), in_specs=[whole((4, 3, LON, 768))...]
    all_to_all x14 -> x6, waiting for transfers between devices: 108 us -> 60.2 us  [swap(): return lax.all_to_all(value, axes, 0, 0, tiled=True)]
    all_to_all x14 -> x6, starting transfers between devices: 84 us -> 43.8 us  [swap(): return lax.all_to_all(value, axes, 0, 0, tiled=True)]
    all_to_all x4, blocking collectives: 102 us -> 128 us  [swap(): return lax.all_to_all(value, axes, 0, 0, tiled=True)]
    ppermute x0 -> x11, waiting for transfers between devices: none -> 24.9 us  [the longest x9 11.1 us: shifted(): return lax.ppermute(value, 'mlp', [(i, (i + by) % 4) for i in range(4)])]
    ppermute x0 -> x11, starting transfers between devices: none -> 22.2 us  [the longest x9 21.8 us: shifted(): return lax.ppermute(value, 'mlp', [(i, (i + by) % 4) for i in range(4)])]
    reduce_scatter x1 -> x2, waiting for transfers between devices: 0.02 us -> 21.8 us  [the longest x1 21.8 us: shards(): share = lax.psum_scatter(share, 'x', scatter_dimension=0, tiled=True)]
  transfers between devices with their start and end apart: 17 -> 21, of which waited for: 14 -> 10; matrix products, arithmetic and copies ran while one was open for 30% -> 7% of each run, Pallas kernels for 0% -> 11%
where the time goes in v2:
time: 469 us; the launch traced here: 462 us
  blocking collectives  128 us (27%)
  waiting for transfers between devices  107 us (23%)
  Pallas kernels  83.9 us (18%)
  starting transfers between devices  66.6 us (14%)
  local copies, waits for them, and re-layouts  42.4 us (9%)
  other arithmetic  18.6 us (4%)
  between operations  14.9 us (3%)
    all_to_all x4, blocking collectives, swap(): return lax.all_to_all(value, axes, 0, 0, tiled=True)  128 us
    all_to_all x6, waiting for transfers between devices, swap(): return lax.all_to_all(value, axes, 0, 0, tiled=True)  60.2 us
    all_to_all x6, starting transfers between devices, swap(): return lax.all_to_all(value, axes, 0, 0, tiled=True)  43.8 us
    ppermute x9, starting transfers between devices, shifted(): return lax.ppermute(value, 'mlp', [(i, (i + by) % 4) for i in range(4)])  21.8 us
    reduce_scatter x1, waiting for transfers between devices, shards(): share = lax.psum_scatter(share, 'x', scatter_dimension=0, tiled=True)  21.8 us
    pallas_call x1, Pallas kernels, chain(): pl.pallas_call(chain_kernel, grid=(4,), in_specs=[whole((4, 3, LON, 768))...  17.7 us
    pallas_call x4, Pallas kernels, transform(): pl.pallas_call(table_kernel, grid=(3,), in_specs=[pl.BlockSpec((384, 1152...  17.1 us
    pallas_call x1, Pallas kernels, weight_grads(): pl.pallas_call(weight_grads_kernel, grid_spec=pltpu.PrefetchScalarGridSpe...  13.9 us
  transfers between devices with their start and end apart: 21, of which 10 were waited for; matrix products, arithmetic and copies ran while one was open for 7% of the time, Pallas kernels for 11%

profile of v2, /device:TPU:1, one launch (start us, length us, event | category | flops | bytes accessed | tf_op | source)
XLA Modules:
  0.0 461.7 jit_solution(12902598470912064363)
XLA Ops:
  8.3 6.9 %collective-permute-start.8 = (bf16[48,768]{1,0:T(8,128)(2,1)S(1)}, bf16[48,768]{1,0:T(8,128)(2,1)S(1)}, u32[]{:S(2)}, u32[]{:S(2)}) collective-permute-start(bf16[48,768]{1,0:T(8,128)(2,1)S(1)} %fusion.1), channel_id=1, source_target_pairs={{0,3},{1,0},{2,1},{3,2},{4,7},{5,4},{6,5},{7,6},{8,11},{9,8},{10,9... | collective-permute-start | bytes 221192 | tf_op jit(solution)/shard_map/ppermute | solution.py:524
  18.5 4.1 collective-permute-done.7
  26.8 7.8 %all-to-all-start = ((bf16[8,144,384]{2,1,0:T(8,128)(2,1)}), bf16[8,144,384]{2,1,0:T(8,128)(2,1)S(1)}, u32[]{:S(2)}, u32[]{:S(2)}) async-start(bf16[8,144,384]{2,1,0:T(8,128)(2,1)} %bitcast), calls=%async_computation | async-start | bytes 1769472 | tf_op jit(solution)/shard_map/all_to_all | solution.py:516
  34.9 18.8 %all-to-all-done = bf16[8,144,384]{2,1,0:T(8,128)(2,1)S(1)} async-done(((bf16[8,144,384]{2,1,0:T(8,128)(2,1)}), bf16[8,144,384]{2,1,0:T(8,128)(2,1)S(1)}, u32[]{:S(2)}, u32[]{:S(2)}) %all-to-all-start) | async-done | bytes 884768 | tf_op jit(solution)/shard_map/all_to_all | solution.py:516
  59.7 5.1 %collective-permute-start.1 = (bf16[2,2,2,96,96]{4,3,2,1,0:T(8,128)(2,1)S(1)}, bf16[2,2,2,96,96]{4,3,2,1,0:T(8,128)(2,1)}, u32[]{:S(2)}, u32[]{:S(2)}) collective-permute-start(bf16[2,2,2,96,96]{4,3,2,1,0:T(8,128)(2,1)S(1)} %pad_maximum_fusion.6), channel_id=1, source_target_pairs={{0,2},{1,3},{2,0},{3,1},{4,6},{5,7},{6,4},{7,5},{8,10},{9,11},{10,... | collective-permute-start | bytes 442376 | tf_op jit(solution)/shard_map/ppermute | solution.py:524
  64.8 4.5 shard_map.345
  69.3 7.0 %all-to-all-start.1 = ((bf16[16,72,384]{2,1,0:T(8,128)(2,1)}), bf16[16,72,384]{2,1,0:T(8,128)(2,1)S(1)}, u32[]{:S(2)}, u32[]{:S(2)}) async-start(bf16[16,72,384]{2,1,0:T(8,128)(2,1)} %bitcast.2), calls=%async_computation.1 | async-start | bytes 1769472 | tf_op jit(solution)/shard_map/all_to_all | solution.py:516
  77.4 6.2 %collective-permute-done = bf16[2,2,2,96,96]{4,3,2,1,0:T(8,128)(2,1)S(1)} collective-permute-done((bf16[2,2,2,96,96]{4,3,2,1,0:T(8,128)(2,1)S(1)}, bf16[2,2,2,96,96]{4,3,2,1,0:T(8,128)(2,1)S(1)}, u32[]{:S(2)}, u32[]{:S(2)}) %collective-permute-start) | collective-permute-done | bytes 147488 | tf_op jit(solution)/shard_map/ppermute | solution.py:524
  97.8 9.2 %shard_map.346 = (bf16[1152,384]{1,0:T(8,128)(2,1)S(1)}, bf16[576,768]{1,0:T(8,128)(2,1)S(1)}, f32[576,768]{1,0:T(8,128)}, bf16[576,768]{1,0:T(8,128)(2,1)S(1)}, f32[576,768]{1,0:T(8,128)}) custom-call(bf16[1152,384]{1,0:T(8,128)(2,1)S(1)} %bitcast.92, bf16[2,576,1152]{2,1,0:T(8,128)(2,1)} %constant.157.clone.fwd.inv_t, ...), custom_call_target="tpu_custom_call" | custom-call | tf_op jit(solution)/shard_map/pallas_call | solution.py:188
  108.0 17.0 %all_to_all.50 = bf16[16,72,384]{2,1,0:T(8,128)(2,1)S(1)} all-to-all(bf16[16,72,384]{2,1,0:T(8,128)(2,1)S(1)} %bitcast.103), channel_id=1, replica_groups=mesh['dp'=2,'x'=4,'y'=4,'core'=2,'mlp'=4] {'x','y'}, dimensions={0} | all-to-all | bytes 1769472 | tf_op jit(solution)/shard_map/all_to_all | solution.py:516
  125.0 4.4 shard_map.347
  129.5 14.7 %all-to-all-start.3 = ((bf16[8,144,384]{2,1,0:T(8,128)(2,1)}), bf16[8,144,384]{2,1,0:T(8,128)(2,1)S(1)}, u32[]{:S(2)}, u32[]{:S(2)}) async-start(bf16[8,144,384]{2,1,0:T(8,128)(2,1)} %bitcast.24), calls=%async_computation.3 | async-start | bytes 1769472 | tf_op jit(solution)/shard_map/all_to_all | solution.py:516
  146.5 16.6 %all-to-all-done.3 = bf16[8,144,384]{2,1,0:T(8,128)(2,1)S(1)} async-done(((bf16[8,144,384]{2,1,0:T(8,128)(2,1)}), bf16[8,144,384]{2,1,0:T(8,128)(2,1)S(1)}, u32[]{:S(2)}, u32[]{:S(2)}) %all-to-all-start.3) | async-done | bytes 884768 | tf_op jit(solution)/shard_map/all_to_all | solution.py:516
  164.1 17.7 %shard_map.348 = (f32[576,768]{1,0:T(8,128)}, bf16[576,768]{1,0:T(8,128)(2,1)S(1)}, bf16[576,768]{1,0:T(8,128)(2,1)S(1)}, bf16[4,576,768]{2,1,0:T(8,128)(2,1)}, ...) custom-call(bf16[4,3,45,768]{3,2,1,0:T(8,128)(2,1)S(1)} %copy.89.x, ...), custom_call_target="tpu_custom_call" | custom-call | tf_op jit(solution)/shard_map/pallas_call | solution.py:360
  181.8 13.9 %shard_map.354 = bf16[2,16,4,48,768]{4,3,2,1,0:T(8,128)(2,1)} custom-call(s32[1]{0:T(128)} %bitcast.39.core, bf16[576,768]{1,0:T(8,128)(2,1)S(1)} %get-tuple-element.49.mixed, bf16[4,576,768]{2,1,0:T(8,128)(2,1)} %get-tuple-element.50.grad_pre, bf16[4,576,768]{2,1,0:T(8,128)(2,1)} %get-tuple-element.39.hidden, bf16[576,768]{1,0:T(8,128)(2,1)S(1)} %get-tuple-element.51.grad_low), custom_call_target="tpu_custom_call" | custom-call | tf_op jit(solution)/shard_map/pallas_call | solution.py:420
  198.7 7.7 %collective-permute-done.9 = bf16[16,4,48,768]{3,2,1,0:T(8,128)(2,1)S(1)} collective-permute-done((bf16[16,4,48,768]{3,2,1,0:T(8,128)(2,1)S(1)}, bf16[16,4,48,768]{3,2,1,0:T(8,128)(2,1)S(1)}, u32[]{:S(2)}, u32[]{:S(2)}) %collective-permute-start.9) | collective-permute-done | bytes 4718624 | tf_op jit(solution)/shard_map/ppermute | solution.py:644
  206.4 3.9 fusion
  210.3 31.8 %all_to_all.51 = bf16[8,144,384]{2,1,0:T(8,128)(2,1)S(1)} all-to-all(bf16[8,144,384]{2,1,0:T(8,128)(2,1)S(1)} %bitcast.101), channel_id=1, replica_groups=mesh['dp'=2,'x'=4,'y'=4,'core'=2,'mlp'=4] {'core','mlp'}, dimensions={0} | all-to-all | bytes 1769472 | tf_op jit(solution)/shard_map/all_to_all | solution.py:516
  242.1 4.5 shard_map.350
  246.6 3.6 all-to-all-start.5
  250.5 21.8 %reduce-scatter.3.cloned.1.call-done = bf16[768,768]{1,0:T(8,128)(2,1)} async-done(((bf16[3072,768]{1,0:T(8,128)(2,1)}), bf16[768,768]{1,0:T(8,128)(2,1)}) %reduce-scatter.3.cloned.1.call-update) | async-done | bytes 1179664 | tf_op jit(solution)/shard_map/reduce_scatter | solution.py:646
  272.4 9.2 %shard_map.351 = (bf16[1152,384]{1,0:T(8,128)(2,1)S(1)}, bf16[576,768]{1,0:T(8,128)(2,1)S(1)}, bf16[576,768]{1,0:T(8,128)(2,1)S(1)}, f32[2,768]{1,0:T(2,128)S(1)}) custom-call(bf16[1152,384]{1,0:T(8,128)(2,1)S(1)} %bitcast.93, bf16[2,576,1152]{2,1,0:T(8,128)(2,1)} %constant.157.clone.fwd.inv_t, bf16[2,1152,576]{2,1,0:T(8,128)(2,1)} %constant.158.clone.inv.fwd_t, ...), custom_call_target="tpu_custom_call" | custom-call | tf_op jit(solution)/shard_map/pallas_call | solution.py:250
  282.5 4.5 shard_map.352
  288.2 5.9 %all-to-all-start.6 = ((bf16[16,104,384]{2,1,0:T(8,128)(2,1)}), bf16[16,104,384]{2,1,0:T(8,128)(2,1)S(1)}, u32[]{:S(2)}, u32[]{:S(2)}) async-start(bf16[16,104,384]{2,1,0:T(8,128)(2,1)} %pad_maximum_fusion.1), calls=%async_computation.6 | async-start | bytes 2555904 | tf_op jit(solution)/shard_map/all_to_all | solution.py:516
  294.2 17.6 %all-to-all-done.6 = bf16[16,104,384]{2,1,0:T(8,128)(2,1)S(1)} async-done(((bf16[16,104,384]{2,1,0:T(8,128)(2,1)}), bf16[16,104,384]{2,1,0:T(8,128)(2,1)S(1)}, u32[]{:S(2)}, u32[]{:S(2)}) %all-to-all-start.6) | async-done | bytes 1277984 | tf_op jit(solution)/shard_map/all_to_all | solution.py:516
  311.9 3.7 shard_map.353
  317.8 52.4 %all_to_all.52 = bf16[8,272,384]{2,1,0:T(8,128)(2,1)S(1)} all-to-all(bf16[8,272,384]{2,1,0:T(8,128)(2,1)S(1)} %pad_maximum_fusion), channel_id=1, replica_groups=mesh['dp'=2,'x'=4,'y'=4,'core'=2,'mlp'=4] {'core','mlp'}, dimensions={0} | all-to-all | bytes 3342336 | tf_op jit(solution)/shard_map/all_to_all | solution.py:516
  371.5 6.1 %collective-permute-done.10 = bf16[2,128,384]{2,1,0:T(8,128)(2,1)S(1)} collective-permute-done((bf16[2,128,384]{2,1,0:T(8,128)(2,1)S(1)}, bf16[2,128,384]{2,1,0:T(8,128)(2,1)S(1)}, u32[]{:S(2)}, u32[]{:S(2)}) %collective-permute-start.10) | collective-permute-done | bytes 196640 | tf_op jit(solution)/shard_map/ppermute | solution.py:681
  385.3 27.3 %all_to_all.53 = f32[16,16,768]{2,1,0:T(8,128)} all-to-all(f32[16,16,768]{2,1,0:T(8,128)S(1)} %broadcast_in_dim.90), channel_id=1, replica_groups=mesh['dp'=2,'x'=4,'y'=4,'core'=2,'mlp'=4] {'dp','core','mlp'}, dimensions={0} | all-to-all | bytes 1572864 | tf_op jit(solution)/shard_map/all_to_all | solution.py:516
  414.7 4.8 %all-to-all-start.9 = ((f32[16,16,768]{2,1,0:T(8,128)}), f32[16,16,768]{2,1,0:T(8,128)}, u32[]{:S(2)}, u32[]{:S(2)}) async-start(f32[16,16,768]{2,1,0:T(8,128)} %broadcast_in_dim.91), calls=%async_computation.11 | async-start | bytes 1572864 | tf_op jit(solution)/shard_map/all_to_all | solution.py:516
  419.6 6.7 %shard_map.349 = bf16[4,3,45,768]{3,2,1,0:T(8,128)(2,1)S(1)} custom-call(bf16[4,576,768]{2,1,0:T(8,128)(2,1)} %get-tuple-element.39.hidden, bf16[32,4,48,768]{3,2,1,0:T(8,128)(2,1)} %bitcast.106, f32[576,768]{1,0:T(8,128)S(1)} %copy-done, f32[576,1]{1,0:T(8,128)S(1)} %reshape.311.present, f32[1,768]{1,0:T(1,128)S(1)} %reshape.274.bias), custom_call_target="tpu_custom_call" | custom-call | tf_op jit(solution)/shard_map/pallas_call | solution.py:457
  429.8 7.0 %all-to-all-done.9 = f32[16,16,768]{2,1,0:T(8,128)} async-done(((f32[16,16,768]{2,1,0:T(8,128)}), f32[16,16,768]{2,1,0:T(8,128)}, u32[]{:S(2)}, u32[]{:S(2)}) %all-to-all-start.9) | async-done | bytes 786464 | tf_op jit(solution)/shard_map/all_to_all | solution.py:516
  (185 shorter events, 74.5 us)
Async XLA Ops:
  7.2 17.0 %copy-start.11 = (bf16[4,3,45,768]{3,0,2,1:T(4,128)(2,1)S(1)}, bf16[4,3,45,768]{3,0,2,1:T(4,128)(2,1)}, u32[]{:S(2)}) copy-start(bf16[4,3,45,768]{3,0,2,1:T(4,128)(2,1)} %param.25) | copy-start | bytes 2488324
  7.2 156.0 %all-gather.5.cloned.1.call-start = ((), (), s32[]{:S(2)}) async-start(), calls=%async_computation.14 | async-start | bytes 9732096 | tf_op jit(solution)/shard_map/all_gather | solution.py:591
  7.2 17.0 %copy-start.15 = (s32[4,3,45]{2,0,1:T(4,128)S(1)}, s32[4,3,45]{2,0,1:T(4,128)}, u32[]{:S(2)}) copy-start(s32[4,3,45]{2,0,1:T(4,128)} %param.26) | copy-start | bytes 6484
  7.3 17.3 %copy-start.16 = (f32[768]{0:T(1024)S(1)}, f32[768]{0:T(1024)}, u32[]{:S(2)}) copy-start(f32[768]{0:T(1024)} %param.27) | copy-start | bytes 9220
  7.3 17.3 %copy-start.17 = (f32[768]{0:T(1024)S(1)}, f32[768]{0:T(1024)}, u32[]{:S(2)}) copy-start(f32[768]{0:T(1024)} %param.28) | copy-start | bytes 9220
  8.3 10.2 %collective-permute-start.8 = (bf16[48,768]{1,0:T(8,128)(2,1)S(1)}, bf16[48,768]{1,0:T(8,128)(2,1)S(1)}, u32[]{:S(2)}, u32[]{:S(2)}) collective-permute-start(bf16[48,768]{1,0:T(8,128)(2,1)S(1)} %fusion.1), channel_id=1, source_target_pairs={{0,3},{1,0},{2,1},{3,2},{4,7},{5,4},{6,5},{7,6},{8,11},{9,8},{10,9... | collective-permute-start | bytes 221192 | tf_op jit(solution)/shard_map/ppermute | solution.py:524
  15.2 7.3 %collective-permute-start.7 = (bf16[48,768]{1,0:T(8,128)(2,1)S(1)}, bf16[48,768]{1,0:T(8,128)(2,1)S(1)}, u32[]{:S(2)}, u32[]{:S(2)}) collective-permute-start(bf16[48,768]{1,0:T(8,128)(2,1)S(1)} %fusion.1), channel_id=1, source_target_pairs={{0,2},{1,3},{2,0},{3,1},{4,6},{5,7},{6,4},{7,5},{8,10},{9,11},{10,... | collective-permute-start | bytes 221192 | tf_op jit(solution)/shard_map/ppermute | solution.py:524
  16.2 7.2 %collective-permute-start.6 = (bf16[48,768]{1,0:T(8,128)(2,1)S(1)}, bf16[48,768]{1,0:T(8,128)(2,1)S(1)}, u32[]{:S(2)}, u32[]{:S(2)}) collective-permute-start(bf16[48,768]{1,0:T(8,128)(2,1)S(1)} %fusion.1), channel_id=1, source_target_pairs={{0,1},{1,2},{2,3},{3,0},{4,5},{5,6},{6,7},{7,4},{8,9},{9,10},{10,1... | collective-permute-start | bytes 221192 | tf_op jit(solution)/shard_map/ppermute | solution.py:524
  24.3 10.5 %copy-start.13 = (bf16[2,2,96,96]{3,2,1,0:T(8,128)(2,1)S(1)}, bf16[2,2,96,96]{3,2,1,0:T(8,128)(2,1)}, u32[]{:S(2)}) copy-start(bf16[2,2,96,96]{3,2,1,0:T(8,128)(2,1)} %param.31) | copy-start | bytes 221188
  24.3 10.5 %copy-start.14 = (bf16[2,2,96,96]{3,2,1,0:T(8,128)(2,1)S(1)}, bf16[2,2,96,96]{3,2,1,0:T(8,128)(2,1)}, u32[]{:S(2)}) copy-start(bf16[2,2,96,96]{3,2,1,0:T(8,128)(2,1)} %param.29) | copy-start | bytes 221188
  26.8 26.9 %all-to-all-start = ((bf16[8,144,384]{2,1,0:T(8,128)(2,1)}), bf16[8,144,384]{2,1,0:T(8,128)(2,1)S(1)}, u32[]{:S(2)}, u32[]{:S(2)}) async-start(bf16[8,144,384]{2,1,0:T(8,128)(2,1)} %bitcast), calls=%async_computation | async-start | bytes 1769472 | tf_op jit(solution)/shard_map/all_to_all | solution.py:516
  53.7 22.5 %collective-permute-start.5 = (f32[1536]{0:T(1024)S(1)}, f32[1536]{0:T(1024)S(1)}, u32[]{:S(2)}, u32[]{:S(2)}) collective-permute-start(f32[1536]{0:T(1024)S(1)} %pad_maximum_fusion.10), channel_id=1, source_target_pairs={{0,3},{1,0},{2,1},{3,2},{4,7},{5,4},{6,5},{7,6},{8,11},{9,8},{10,9... | collective-permute-start | bytes 18440 | tf_op jit(solution)/shard_map/ppermute | solution.py:524
  55.8 21.1 %collective-permute-start.4 = (f32[1536]{0:T(1024)S(1)}, f32[1536]{0:T(1024)S(1)}, u32[]{:S(2)}, u32[]{:S(2)}) collective-permute-start(f32[1536]{0:T(1024)S(1)} %pad_maximum_fusion.10), channel_id=1, source_target_pairs={{0,2},{1,3},{2,0},{3,1},{4,6},{5,7},{6,4},{7,5},{8,10},{9,11},{10,... | collective-permute-start | bytes 18440 | tf_op jit(solution)/shard_map/ppermute | solution.py:524
  56.1 20.8 %collective-permute-start.3 = (f32[1536]{0:T(1024)S(1)}, f32[1536]{0:T(1024)S(1)}, u32[]{:S(2)}, u32[]{:S(2)}) collective-permute-start(f32[1536]{0:T(1024)S(1)} %pad_maximum_fusion.10), channel_id=1, source_target_pairs={{0,1},{1,2},{2,3},{3,0},{4,5},{5,6},{6,7},{7,4},{8,9},{9,10},{10,1... | collective-permute-start | bytes 18440 | tf_op jit(solution)/shard_map/ppermute | solution.py:524
  58.2 19.1 %collective-permute-start.2 = (bf16[2,2,2,96,96]{4,3,2,1,0:T(8,128)(2,1)S(1)}, bf16[2,2,2,96,96]{4,3,2,1,0:T(8,128)(2,1)S(1)}, u32[]{:S(2)}, u32[]{:S(2)}) collective-permute-start(bf16[2,2,2,96,96]{4,3,2,1,0:T(8,128)(2,1)S(1)} %pad_maximum_fusion.6), channel_id=1, source_target_pairs={{0,3},{1,0},{2,1},{3,2},{4,7},{5,4},{6,5},{7,6},{8,11},{9,8},{10,9... | collective-permute-start | bytes 442376 | tf_op jit(solution)/shard_map/ppermute | solution.py:524
  59.7 17.7 %collective-permute-start.1 = (bf16[2,2,2,96,96]{4,3,2,1,0:T(8,128)(2,1)S(1)}, bf16[2,2,2,96,96]{4,3,2,1,0:T(8,128)(2,1)}, u32[]{:S(2)}, u32[]{:S(2)}) collective-permute-start(bf16[2,2,2,96,96]{4,3,2,1,0:T(8,128)(2,1)S(1)} %pad_maximum_fusion.6), channel_id=1, source_target_pairs={{0,2},{1,3},{2,0},{3,1},{4,6},{5,7},{6,4},{7,5},{8,10},{9,11},{10,... | collective-permute-start | bytes 442376 | tf_op jit(solution)/shard_map/ppermute | solution.py:524
  69.3 28.6 %all-to-all-start.1 = ((bf16[16,72,384]{2,1,0:T(8,128)(2,1)}), bf16[16,72,384]{2,1,0:T(8,128)(2,1)S(1)}, u32[]{:S(2)}, u32[]{:S(2)}) async-start(bf16[16,72,384]{2,1,0:T(8,128)(2,1)} %bitcast.2), calls=%async_computation.1 | async-start | bytes 1769472 | tf_op jit(solution)/shard_map/all_to_all | solution.py:516
  76.3 7.3 %collective-permute-start = (bf16[2,2,2,96,96]{4,3,2,1,0:T(8,128)(2,1)S(1)}, bf16[2,2,2,96,96]{4,3,2,1,0:T(8,128)(2,1)S(1)}, u32[]{:S(2)}, u32[]{:S(2)}) collective-permute-start(bf16[2,2,2,96,96]{4,3,2,1,0:T(8,128)(2,1)S(1)} %pad_maximum_fusion.6), channel_id=1, source_target_pairs={{0,1},{1,2},{2,3},{3,0},{4,5},{5,6},{6,7},{7,4},{8,9},{9,10},{10,1... | collective-permute-start | bytes 442376 | tf_op jit(solution)/shard_map/ppermute | solution.py:524
  129.5 17.0 %copy-start.18 = (f32[768]{0:T(1024)S(1)}, f32[768]{0:T(1024)}, u32[]{:S(2)}) copy-start(f32[768]{0:T(1024)} %param.33) | copy-start | bytes 9220
  129.5 17.0 %copy-start.19 = (f32[768]{0:T(1024)S(1)}, f32[768]{0:T(1024)}, u32[]{:S(2)}) copy-start(f32[768]{0:T(1024)} %param.34) | copy-start | bytes 9220
  129.5 33.7 %all-to-all-start.3 = ((bf16[8,144,384]{2,1,0:T(8,128)(2,1)}), bf16[8,144,384]{2,1,0:T(8,128)(2,1)S(1)}, u32[]{:S(2)}, u32[]{:S(2)}) async-start(bf16[8,144,384]{2,1,0:T(8,128)(2,1)} %bitcast.24), calls=%async_computation.3 | async-start | bytes 1769472 | tf_op jit(solution)/shard_map/all_to_all | solution.py:516
  144.1 128.2 %reduce-scatter.3.cloned.1.call-start = ((), (), s32[]{:S(2)}) async-start(), calls=%async_computation.12 | async-start | bytes 5898240 | tf_op jit(solution)/shard_map/reduce_scatter | solution.py:646
  195.6 10.8 %copy-start.8 = (bf16[2,16,4,48,768]{4,3,2,1,0:T(8,128)(2,1)S(1)}, bf16[2,16,4,48,768]{4,3,2,1,0:T(8,128)(2,1)}, u32[]{:S(2)}) copy-start(bf16[2,16,4,48,768]{4,3,2,1,0:T(8,128)(2,1)} %shard_map.354) | copy-start | bytes 28311556
  198.4 8.0 %collective-permute-start.9 = (bf16[16,4,48,768]{3,2,1,0:T(8,128)(2,1)S(1)}, bf16[16,4,48,768]{3,2,1,0:T(8,128)(2,1)S(1)}, u32[]{:S(2)}, u32[]{:S(2)}) collective-permute-start(bf16[16,4,48,768]{3,2,1,0:T(8,128)(2,1)S(1)} %slice_bitcast_fusion), channel_id=1, source_target_pairs={{0,4},{4,0},{1,5},{5,1},{2,6},{6,2},{3,7},{7,3},{8,12},{12,8},{9,1... | collective-permute-start | bytes 14155784 | tf_op jit(solution)/shard_map/ppermute | solution.py:644
  246.6 25.7 %all-to-all-start.5 = ((bf16[16,72,384]{2,1,0:T(8,128)(2,1)}), bf16[16,72,384]{2,1,0:T(8,128)(2,1)S(1)}, u32[]{:S(2)}, u32[]{:S(2)}) async-start(bf16[16,72,384]{2,1,0:T(8,128)(2,1)} %bitcast.33), calls=%async_computation.5 | async-start | bytes 1769472 | tf_op jit(solution)/shard_map/all_to_all | solution.py:516
  250.2 65.5 %reduce-scatter.5.cloned.1.call-start = ((), (), s32[]{:S(2)}) async-start(), calls=%async_computation.13 | async-start | bytes 1474560 | tf_op jit(solution)/shard_map/reduce_scatter | solution.py:647
  288.2 23.7 %all-to-all-start.6 = ((bf16[16,104,384]{2,1,0:T(8,128)(2,1)}), bf16[16,104,384]{2,1,0:T(8,128)(2,1)S(1)}, u32[]{:S(2)}, u32[]{:S(2)}) async-start(bf16[16,104,384]{2,1,0:T(8,128)(2,1)} %pad_maximum_fusion.1), calls=%async_computation.6 | async-start | bytes 2555904 | tf_op jit(solution)/shard_map/all_to_all | solution.py:516
  294.1 149.1 %all-gather.7.cloned.1.call-start = ((), (), s32[]{:S(2)}) async-start(), calls=%async_computation.15 | async-start | bytes 3342336 | tf_op jit(solution)/shard_map/all_gather | solution.py:683
  371.4 6.2 %collective-permute-start.10 = (bf16[2,128,384]{2,1,0:T(8,128)(2,1)S(1)}, bf16[2,128,384]{2,1,0:T(8,128)(2,1)S(1)}, u32[]{:S(2)}, u32[]{:S(2)}) collective-permute-start(bf16[2,128,384]{2,1,0:T(8,128)(2,1)S(1)} %bitcast_reduce_fusion), channel_id=1, source_target_pairs={{0,128},{128,0},{1,129},{129,1},{2,130},{130,2},{3,131},{131,3},{4... | collective-permute-start | bytes 589832 | tf_op jit(solution)/shard_map/ppermute | solution.py:681
  385.3 34.2 %copy-start.20 = (f32[768]{0:T(1024)S(1)}, f32[768]{0:T(1024)}, u32[]{:S(2)}) copy-start(f32[768]{0:T(1024)} %param.38) | copy-start | bytes 9220
  385.3 34.2 %copy-start = (f32[576,768]{1,0:T(8,128)S(1)}, f32[576,768]{1,0:T(8,128)}, u32[]{:S(2)}) copy-start(f32[576,768]{1,0:T(8,128)} %get-tuple-element.40.stream) | copy-start | bytes 5308420
  414.7 22.2 %all-to-all-start.9 = ((f32[16,16,768]{2,1,0:T(8,128)}), f32[16,16,768]{2,1,0:T(8,128)}, u32[]{:S(2)}, u32[]{:S(2)}) async-start(f32[16,16,768]{2,1,0:T(8,128)} %broadcast_in_dim.91), calls=%async_computation.11 | async-start | bytes 1572864 | tf_op jit(solution)/shard_map/all_to_all | solution.py:516
  (13 other events, 75.6 us)
Sparse Core Ops, SparseCore 0:
  24.3 66.5 all-gather.4
  210.5 61.7 reduce-scatter.2
  274.9 39.3 reduce-scatter.4
  378.5 53.9 all-gather.6

commit v3 on v2

--- a/solution.py
+++ b/solution.py
@@ -71,8 +71,8 @@
 def block_fold():
     at = np.arange(384) // 96
     mask = (at[:, None] == at[None, :]).astype(np.float32)
-    fold = np.tile(np.eye(96, 128), (4, 1))
-    return mask, fold.astype(np.float32).astype(bf16)
+    fold = np.tile(np.eye(96, 128), (4, 1)).astype(np.float32)
+    return mask.astype(bf16), fold.astype(bf16)
 
 
 def mm(left, right):
@@ -104,10 +104,6 @@
     return rows[...]
 
 
-def both_halves(pair, s):
-    return jnp.concatenate([pair[0, s], pair[1, s]], axis=-1).astype(f32)
-
-
 def whole(shape):
     return pl.BlockSpec(shape, lambda *_: (0,) * len(shape))
 
@@ -116,29 +112,63 @@
     return jax.ShapeDtypeStruct(shape, dtype)
 
 
+def pack(first, second, m):
+    here = slice(192 * m, 192 * m + 192)
+    return jnp.concatenate([first[:, here], second[:, here]], axis=1)
+
+
+def unpack(pieces, r, s2):
+    here = slice(192 * s2, 192 * s2 + 192)
+    return jnp.concatenate([pieces[r, m][:, here] for m in range(4)], axis=1).astype(f32)
+
+
 def norm_kernel(x, present, gain, shift, out, rows):
     rows[...] = jnp.zeros_like(rows)
-    normed, _ = standard(widen(rows, x.at[0]))
-    masked = ((normed * gain[...] + shift[...]) * present[...]).astype(bf16)
-    out[0, 0] = masked[:, :384]
-    out[1, 0] = masked[:, 384:]
+    pair = []
+    for s2 in range(2):
+        normed, _ = standard(widen(rows, x.at[s2]))
+        here = slice(144 * s2, 144 * s2 + 144)
+        pair.append(((normed * gain[...] + shift[...]) * present[here]).astype(bf16))
+    for m in range(4):
+        out[0, m] = pack(pair[0], pair[1], m)
 
 
 def norm_pack(inputs, present, gain, shift):
     return pl.pallas_call(
         norm_kernel,
-        grid=(4,),
+        grid=(2,),
         in_specs=[
-            pl.BlockSpec((1, 3, LON, 768), lambda s: (s, 0, 0, 0)),
-            pl.BlockSpec((144, 1), lambda s: (s, 0)),
-            whole((1, 768)),
-            whole((1, 768)),
-        ],
-        out_specs=pl.BlockSpec((2, 1, 144, 384), lambda s: (0, s, 0, 0)),
+            pl.BlockSpec((2, 3, LON, 768), lambda r: (r, 0, 0, 0)),
+            pl.BlockSpec((288, 1), lambda r: (r, 0)),
+            whole((1, 768)),
+            whole((1, 768)),
+        ],
+        out_specs=pl.BlockSpec((1, 4, 144, 384), lambda r: (r, 0, 0, 0)),
         out_shape=struct((2, 4, 144, 384), bf16),
         scratch_shapes=[pltpu.VMEM((144, 768), f32)],
         compiler_params=ROOM,
     )(inputs, present, gain, shift)
+
+
+def mix_kernel(w_in, w_out, mask, mix_in, mix_out):
+    for source, out in ((w_in, mix_in), (w_out, mix_out)):
+        parts = []
+        for part in range(2):
+            row = jnp.concatenate([source[part, 0], source[part, 1]], axis=1)
+            row = jnp.concatenate([row, row], axis=1)
+            parts.append(jnp.concatenate([row] * 4, axis=0) * mask[...])
+        out[:384, :384] = parts[0]
+        out[384:, 384:] = parts[0]
+        out[:384, 384:] = parts[1]
+        out[384:, :384] = -parts[1]
+
+
+def mixers(w_in, w_out, mask):
+    return pl.pallas_call(
+        mix_kernel,
+        out_shape=[struct((768, 768), bf16)] * 2,
+        compiler_params=ROOM,
+    )(w_in, w_out, mask)
 
 
 def table_kernel(table, rows, out):
@@ -277,19 +307,20 @@
         real = grad[:384, :384] + grad[384:, 384:]
         imag = grad[:384, 384:] - grad[384:, :384]
         for part, value in enumerate((real, imag)):
-            blocks = mm((value * mask[...]).astype(bf16), fold[...]).astype(bf16)
+            value = value * mask[...].astype(f32)
+            blocks = mm((value[:192] + value[192:]).astype(bf16), fold[...]).astype(bf16)
             for piece in range(3):
-                at = which * 768 + part * 384 + piece * 128
-                group, row = at // 256, at % 256
-                out[row : row + 128, group * 128 : group * 128 + 128] = blocks[
-                    piece * 128 : piece * 128 + 128
+                at = which * 384 + part * 192 + piece * 64
+                group, row = at // 128, at % 128
+                out[row : row + 64, group * 128 : group * 128 + 128] = blocks[
+                    piece * 64 : piece * 64 + 64
                 ]
 
 
 def filter_grads(low, first_low, active, second_low, mask, fold):
     return pl.pallas_call(
         filter_grads_kernel,
-        out_shape=struct((256, 768), bf16),
+        out_shape=struct((128, 768), bf16),
         compiler_params=ROOM,
     )(low, first_low, active, second_low, mask, fold)
 
@@ -312,7 +343,7 @@
             value = widen(rows, x.at[s])
             first, _ = standard(value)
             masked = (first * gain_first[...] + shift_first[...]) * there
-            value = value + both_halves(filtered, s) + masked
+            value = value + unpack(filtered, s // 2, s % 2) + masked
             stream[here] = value
             value, spread_of = standard(value.astype(bf16).astype(f32))
             normed[here] = value
@@ -339,6 +370,7 @@
 
     @pl.when(step == 3)
     def _():
+        lows = []
         for s in range(4):
             here = slice(144 * s, 144 * s + 144)
             grad = total[here]
@@ -351,8 +383,10 @@
             )
             grad = widen(rows, cotangent.at[s]) + scale[here] * grad
             grad_stream[here] = grad
-            packed[0, s] = grad[:, :384].astype(bf16)
-            packed[1, s] = grad[:, 384:].astype(bf16)
+            lows.append(grad.astype(bf16))
+        for r in range(2):
+            for m in range(4):
+                packed[r, m] = pack(lows[2 * r], lows[2 * r + 1], m)
 
 
 def chain(x, present, filtered, cotangent, gain_first, shift_first, gain, shift, weights, units):
@@ -405,31 +439,26 @@
     )(x, present, filtered, cotangent, gain_first, shift_first, gain, shift, weights, weights, units)
 
 
-def weight_grads_kernel(core, mixed, grad_pre, hidden, grad_low, out):
+def weight_grads_kernel(mixed, grad_pre, hidden, grad_low, out):
     @pl.when(pl.program_id(1) == 0)
     def _():
-        out[...] = inner_rows(mixed[...], grad_pre[0]).astype(bf16).reshape(1, 16, 1, PAD, 768)
+        out[...] = inner_rows(mixed[...], grad_pre[0]).astype(bf16).reshape(16, 1, 1, PAD, 768)
 
     @pl.when(pl.program_id(1) == 1)
     def _():
-        out[...] = inner_rows(hidden[0], grad_low[...]).astype(bf16).reshape(1, 16, 1, PAD, 768)
-
-
-def weight_grads(core, mixed, grad_pre, hidden, grad_low):
-    group = pl.BlockSpec((1, 576, 768), lambda g, w, c: (g, 0, 0))
+        out[...] = inner_rows(hidden[0], grad_low[...]).astype(bf16).reshape(16, 1, 1, PAD, 768)
+
+
+def weight_grads(mixed, grad_pre, hidden, grad_low):
+    group = pl.BlockSpec((1, 576, 768), lambda g, w: (g, 0, 0))
     return pl.pallas_call(
         weight_grads_kernel,
-        grid_spec=pltpu.PrefetchScalarGridSpec(
-            num_scalar_prefetch=1,
-            grid=(4, 2),
-            in_specs=[whole((576, 768)), group, group, whole((576, 768))],
-            out_specs=pl.BlockSpec(
-                (1, 16, 1, PAD, 768), lambda g, w, c: ((w + c[0]) % 2, 0, g, 0, 0)
-            ),
-        ),
-        out_shape=struct((2, 16, 4, PAD, 768), bf16),
-        compiler_params=ROOM,
-    )(core, mixed, grad_pre, hidden, grad_low)
+        grid=(4, 2),
+        in_specs=[whole((576, 768)), group, group, whole((576, 768))],
+        out_specs=pl.BlockSpec((16, 1, 1, PAD, 768), lambda g, w: (0, w, g, 0, 0)),
+        out_shape=struct((16, 2, 4, PAD, 768), bf16),
+        compiler_params=ROOM,
+    )(mixed, grad_pre, hidden, grad_low)
 
 
 def output_kernel(hidden, w_out, stream, present, bias, out, total):
@@ -477,33 +506,35 @@
         sums[...] = jnp.zeros_like(sums)
 
     rows[...] = jnp.zeros_like(rows)
-    normed, scale = standard(widen(rows, x.at[0]))
-    stream = grad_stream[...]
-    grad = (both_halves(from_spec, 0) + stream) * present[...]
-    sums[0:1, :] += jnp.sum(grad * normed, axis=0, keepdims=True)
-    sums[1:2, :] += jnp.sum(grad, axis=0, keepdims=True)
-    grad = grad * gain[...]
-    grad = grad - jnp.mean(grad, axis=-1, keepdims=True) - normed * jnp.mean(
-        grad * normed, axis=-1, keepdims=True
-    )
-    grad = stream + scale * grad
-    for i in range(3):
-        out[0, i] = grad[PAD * i : PAD * i + LON]
+    for s2 in range(2):
+        here = slice(144 * s2, 144 * s2 + 144)
+        normed, scale = standard(widen(rows, x.at[s2]))
+        stream = grad_stream[here]
+        grad = (unpack(from_spec, 0, s2) + stream) * present[here]
+        sums[0:1, :] += jnp.sum(grad * normed, axis=0, keepdims=True)
+        sums[1:2, :] += jnp.sum(grad, axis=0, keepdims=True)
+        grad = grad * gain[...]
+        grad = grad - jnp.mean(grad, axis=-1, keepdims=True) - normed * jnp.mean(
+            grad * normed, axis=-1, keepdims=True
+        )
+        grad = stream + scale * grad
+        for i in range(3):
+            out[s2, i] = grad[PAD * i : PAD * i + LON]
 
 
 def input_grads(x, present, from_spec, grad_stream, gain):
     return pl.pallas_call(
         final_kernel,
-        grid=(4,),
+        grid=(2,),
         in_specs=[
-            pl.BlockSpec((1, 3, LON, 768), lambda s: (s, 0, 0, 0)),
-            pl.BlockSpec((144, 1), lambda s: (s, 0)),
-            pl.BlockSpec((2, 1, 144, 384), lambda s: (0, s, 0, 0)),
-            pl.BlockSpec((144, 768), lambda s: (s, 0)),
+            pl.BlockSpec((2, 3, LON, 768), lambda r: (r, 0, 0, 0)),
+            pl.BlockSpec((288, 1), lambda r: (r, 0)),
+            pl.BlockSpec((1, 4, 144, 384), lambda r: (r, 0, 0, 0)),
+            pl.BlockSpec((288, 768), lambda r: (r, 0)),
             whole((1, 768)),
         ],
         out_specs=[
-            pl.BlockSpec((1, 3, LON, 768), lambda s: (s, 0, 0, 0)),
+            pl.BlockSpec((2, 3, LON, 768), lambda r: (r, 0, 0, 0)),
             whole((2, 768)),
         ],
         out_shape=[struct((4, 3, LON, 768), f32), struct((2, 768), f32)],
@@ -512,14 +543,90 @@
     )(x, present, from_spec, grad_stream, gain)
 
 
+def gather_kernel(rows, out):
+    near = rows[...].astype(f32)
+    near = near[0] + near[1]
+    every = near[0] + near[1] + near[2] + near[3]
+    small = jnp.concatenate(
+        [every[56:65]] + [near[m, 65:66] for m in range(4)] + [jnp.zeros((3, 768), f32)], axis=0
+    )
+    value = jnp.concatenate(
+        [every[:PAD]] + [near[m, PAD : PAD + 8] for m in range(4)] + [small], axis=0
+    ).astype(bf16)
+    for q in range(16):
+        out[q] = value
+
+
+def gather_rows(rows):
+    return pl.pallas_call(
+        gather_kernel,
+        out_shape=struct((16, 96, 768), bf16),
+        compiler_params=ROOM,
+    )(rows)
+
+
+def finish_kernel(place, own, other, w_in, w_out, f_in, f_out, small, units, biases):
+    core, group = place[0], place[1]
+    own_share = own[:, :PAD].reshape(768, 768).astype(f32)
+    other_share = other[:, :PAD].reshape(768, 768).astype(f32)
+
+    @pl.when(core == 0)
+    def _():
+        w_in[...] = own_share
+        w_out[...] = other_share
+
+    @pl.when(core == 1)
+    def _():
+        w_in[...] = other_share
+        w_out[...] = own_share
+
+    rest = own[:, PAD:].astype(f32) + other[:, PAD:].astype(f32)
+    for m in range(4):
+        rows = rest[:, 8 * m : 8 * m + 8].reshape(128, 768)
+        for which, out in enumerate((f_in, f_out)):
+            for part in range(2):
+                for b in range(2):
+                    pieces = []
+                    for piece in range(3):
+                        at = which * 384 + part * 192 + b * 96 + piece * 32
+                        u, row = at // 128, at % 128
+                        pieces.append(rows[row : row + 32, 128 * u : 128 * u + 128])
+                    out[part, 2 * m + b] = jnp.concatenate(pieces, axis=0)[:, :96]
+    sums = jnp.sum(rest[:, 32:], axis=0)
+    small[...] = jnp.zeros_like(small)
+    for k in range(4):
+
+        @pl.when(group == k)
+        def _():
+            small[0:5, :] = sums[0:5, 192 * k : 192 * k + 192]
+            units[...] = sums[5 + k : 6 + k]
+
+    biases[...] = sums[9:13]
+
+
+def finish(place, own, other):
+    vmem = pl.BlockSpec(memory_space=pltpu.VMEM)
+    return pl.pallas_call(
+        finish_kernel,
+        in_specs=[pl.BlockSpec(memory_space=pltpu.SMEM), vmem, vmem],
+        out_specs=[vmem] * 7,
+        out_shape=[
+            struct((768, 768), f32),
+            struct((768, 768), f32),
+            struct((2, 8, 96, 96), f32),
+            struct((2, 8, 96, 96), f32),
+            struct((8, 192), f32),
+            struct((1, 768), f32),
+            struct((4, 768), f32),
+        ],
+        compiler_params=ROOM,
+    )(place, own, other)
+
+
 def swap(value, axes):
     return lax.all_to_all(value, axes, 0, 0, tiled=True)
 
 
-def spread(value, axes, count):
-    return swap(jnp.broadcast_to(value[None], (count,) + value.shape), axes)
-
-
 def shifted(value, by):
     return lax.ppermute(value, "mlp", [(i, (i + by) % 4) for i in range(4)])
 
@@ -530,28 +637,6 @@
 
 def narrow(rows):
     return jnp.concatenate([rows[..., :384], rows[..., 384:]], axis=-2)
-
-
-def broad(rows):
-    n = rows.shape[-2] // 2
-    return jnp.concatenate([rows[..., :n, :], rows[..., n:, :]], axis=-1)
-
-
-def block_form(weights):
-    eye = jnp.eye(4, dtype=weights.dtype)
-    dense = jnp.einsum("pbef,bc->pbecf", weights, eye).reshape(2, 384, 384)
-    return jnp.concatenate(
-        [
-            jnp.concatenate([dense[0], dense[1]], axis=1),
-            jnp.concatenate([-dense[1], dense[0]], axis=1),
-        ],
-        axis=0,
-    )
-
-
-def total_of(vector):
-    near = jnp.sum(spread(vector, ("dp", "core", "mlp"), 16), axis=0)
-    return jnp.sum(spread(near, XY, 16), axis=0)
 
 
 def after(value, *others):
@@ -585,34 +670,33 @@
     )
 
     wide = lax.axis_index(("x", "y", "core"))
+    high = lax.reduce_precision(bias_in, 8, 7)
+    middle = lax.reduce_precision(bias_in - high, 8, 7)
+    bias_rows = jnp.stack([high, middle, bias_in - high - middle]).astype(bf16)
     both = jnp.concatenate([weight_in, weight_out], axis=0)
-    piece = lax.dynamic_slice_in_dim(both, wide * PAD, PAD, 0)
-    piece = jnp.stack([piece] + [shifted(piece, d) for d in (1, 2, 3)])
-    weights = lax.all_gather(piece, ("x", "y", "core"))
+    piece = jnp.concatenate(
+        [
+            lax.dynamic_slice_in_dim(both, wide * PAD, PAD, 0),
+            bias_rows,
+            jnp.zeros((13, 768), bf16),
+        ]
+    )
+    pieces = jnp.stack([piece] + [shifted(piece, d) for d in (1, 2, 3)])
 
     present = jnp.pad(validity.astype(f32), ((0, 0), (0, 0), (0, PAD - LON))).reshape(576, 1)
     packed = norm_pack(inputs, present, gain_first, shift_first)
     tokens = swap(packed.reshape(8, 144, 384), PAIR)
 
-    small = after(
-        jnp.concatenate([bias_in, spectral_in_bias.reshape(-1), spectral_out_bias.reshape(-1)]), tokens
-    )
-    filters = after(jnp.stack([spectral_in, spectral_out]), tokens)
-    small = jnp.stack([small] + [shifted(small, d) for d in (1, 2, 3)])
-    filters = jnp.stack([filters] + [shifted(filters, d) for d in (1, 2, 3)])
-
-    def my_half(value):
-        pair = [
-            lax.dynamic_index_in_dim(value, (group - 2 * core - u) % 4, 0, keepdims=False)
-            for u in range(2)
-        ]
-        return jnp.concatenate(pair, axis=1)
-
-    units = small[:, :768].reshape(4, 1, 768)
-    mix_in = block_form(my_half(filters[:, 0]))
-    mix_out = block_form(my_half(filters[:, 1]))
-    mix_in_bias = my_half(small[:, 768:1152].reshape(4, 2, 2, 96)).reshape(1, 768)
-    mix_out_bias = my_half(small[:, 1152:].reshape(4, 2, 2, 96)).reshape(1, 768)
+    pieces = after(pieces, tokens)
+    weights = lax.all_gather(pieces[:, :PAD], ("x", "y", "core"))
+    units = pieces[:, PAD : PAD + 3].astype(f32)
+    units = (units[:, 0] + units[:, 1] + units[:, 2]).reshape(4, 1, 768)
+
+    mix_in, mix_out = mixers(spectral_in, spectral_out, mask)
+    mix_in_bias, mix_out_bias = (
+        jnp.tile(value.reshape(2, 1, 192), (1, 2, 1)).reshape(1, 768)
+        for value in (spectral_in_bias, spectral_out_bias)
+    )
 
     spectrum = transform(table["lon_fwd"], tokens.reshape(1152, 384))
     back, grid_low, first, active, second = filter_forward(
@@ -639,12 +723,9 @@
         weights,
         units,
     )
+    share = weight_grads(mixed, grad_pre, hidden, grad_low).reshape(6144, 768)
+    share = lax.psum_scatter(share, ("x", "y", "core"), scatter_dimension=0, tiled=True)
     tokens = swap(packed.reshape(8, 144, 384), PAIR)
-    slots = weight_grads(core.astype(jnp.int32).reshape(1), mixed, grad_pre, hidden, grad_low)
-    taken = lax.ppermute(slots[1], "core", [(0, 1), (1, 0)])
-    share = (slots[0].astype(f32) + taken.astype(f32)).astype(bf16).reshape(3072, 768)
-    share = lax.psum_scatter(share, "x", scatter_dimension=0, tiled=True)
-    share = lax.psum_scatter(share, "y", scatter_dimension=0, tiled=True)
     output = layer_output(hidden, weights, stream, present, bias_out)
 
     grad_columns = across(transform(table["lon_inv_t"], tokens.reshape(1152, 384)))
@@ -654,71 +735,49 @@
     filter_share = filter_grads(grid_low, first_low, active, second_low, mask, fold)
     joined = swap(
         jnp.concatenate(
-            [grad_spectrum.reshape(16, 72, 384), narrow(filter_share.reshape(16, 16, 768))], axis=1
+            [grad_spectrum.reshape(16, 72, 384), narrow(filter_share.reshape(16, 8, 768))], axis=1
         ),
         XY,
     )
     grad_rows = joined[:, :72].reshape(1152, 384)
     filter_share = jnp.sum(joined[:, 72:].astype(f32), axis=0).astype(bf16)
+    filter_share = jnp.concatenate([filter_share[:8], filter_share[8:]], axis=1)
     from_spec = transform(table["lon_fwd_t"], grad_rows)
+    from_spec = swap(from_spec.reshape(8, 144, 384), PAIR).reshape(2, 4, 144, 384)
+    grad_inputs, first_sums = input_grads(inputs, present, from_spec, grad_stream, gain_first)
 
     order = (group - jnp.arange(4, dtype=jnp.int32)) % 4
-    share = jnp.take(narrow(share.reshape(4, PAD, 768)), order, axis=0)
-    share = jnp.broadcast_to(share[None], (2, 4, 96, 384)).reshape(8, 96, 384)
-    joined = swap(
-        jnp.concatenate(
-            [
-                from_spec.reshape(8, 144, 384),
-                share,
-                jnp.broadcast_to(filter_share[None], (8, 32, 384)),
-            ],
-            axis=1,
-        ),
-        PAIR,
-    )
-    from_spec = joined[:, :144].reshape(2, 4, 144, 384)
-    share = jnp.sum(joined[:, 144:].reshape(2, 4, 128, 384).astype(f32), axis=1).astype(bf16)
-    other = lax.ppermute(share, "dp", [(0, 1), (1, 0)])
-    share = (share.astype(f32) + other.astype(f32)).astype(bf16)
-    gathered = lax.all_gather(share, XY)
-    grad_slices = broad(gathered[:, :, :96]).swapaxes(0, 1).reshape(2, 768, 768).astype(f32)
-    filters = broad(gathered[:, :, 96:]).reshape(16, 2, 16, 6, 128)[..., :96]
-    filters = filters.transpose(1, 3, 0, 2, 4).reshape(2, 2, 2, 4, 96, 96)
-    filters = filters.transpose(1, 2, 0, 3, 4, 5).reshape(2, 2, 8, 96, 96).astype(f32)
-
-    grad_inputs, first_sums = input_grads(inputs, present, from_spec, grad_stream, gain_first)
-
-    filter_sums = filter_sums.reshape(2, 2, 1, 384)
-    filter_sums = jnp.where(
-        core == jnp.arange(2, dtype=jnp.int32)[None, None, :, None], filter_sums, 0.0
-    )
     unit_sums = jnp.take(unit_sums.reshape(4, 768), order, axis=0)
-    small = total_of(
-        jnp.concatenate(
-            [first_sums, sums, unit_sums, filter_sums.reshape(4, 768), jnp.zeros((3, 768), f32)]
-        )
-    )
-    filter_sums = small[9:13].reshape(2, 2, 8, 96)
-    unit_sums = lax.dynamic_index_in_dim(small[5:9], group, 0, keepdims=False)
-
-    def mine(vector):
-        return lax.dynamic_slice_in_dim(vector, group * 192, 192, 0)
-
+    filter_sums = jnp.sum(filter_sums.reshape(2, 2, 2, 192), axis=2).reshape(1, 768)
+    small = jnp.concatenate(
+        [first_sums, sums, unit_sums, filter_sums, jnp.zeros((6, 768), f32)]
+    ).astype(bf16)
+    share = jnp.take(share.reshape(4, PAD, 768), order, axis=0)
+    rest = jnp.concatenate([filter_share, small])
+    rows = jnp.concatenate([share, jnp.broadcast_to(rest[None], (4, 24, 768))], axis=1)
+    rows = jnp.broadcast_to(rows[None], (2, 4, 72, 768)).reshape(8, 72, 768)
+    rows = swap(rows, ("dp", "mlp")).reshape(2, 4, 72, 768)
+    rows = swap(gather_rows(rows), XY)
+    other = lax.ppermute(rows, "core", [(0, 1), (1, 0)])
+    grad_w_in, grad_w_out, grad_f_in, grad_f_out, small, unit_sums, biases = finish(
+        jnp.stack([core, group]).astype(jnp.int32), rows, other
+    )
+    biases = biases.reshape(4, 2, 2, 2, 96).transpose(1, 2, 0, 3, 4).reshape(2, 2, 8, 96)
     return (
         output,
         grad_inputs,
-        mine(small[0]),
-        mine(small[1]),
-        filters[0],
-        filter_sums[0],
-        filters[1],
-        filter_sums[1],
-        mine(small[2]),
-        mine(small[3]),
-        grad_slices[0],
-        unit_sums,
-        grad_slices[1],
-        mine(small[4]),
+        small[0],
+        small[1],
+        grad_f_in,
+        biases[0],
+        grad_f_out,
+        biases[1],
+        small[2],
+        small[3],
+        grad_w_in,
+        unit_sums.reshape(768),
+        grad_w_out,
+        small[4],
     )
 
 

time: 469 us -> 408 us (0.87); the launches traced: 462 us -> 407 us
  waiting for transfers between devices: 107 us -> 73.5 us
  blocking collectives: 128 us -> 158 us
  local copies, waits for them, and re-layouts: 42.4 us -> 21 us
  starting transfers between devices: 66.6 us -> 49.3 us
  other arithmetic: 18.6 us -> 2.84 us
    all_to_all x4 -> x6, blocking collectives: 128 us -> 158 us  [swap(): return lax.all_to_all(value, axes, 0, 0, tiled=True)]
    reduce_scatter x2 -> x1, waiting for transfers between devices: 21.8 us -> 0.02 us  [shards(): lax.psum_scatter(share, ('x', 'y', 'core'), scatter_dimension=0, tiled=True)]
    ppermute x9 -> x3, starting transfers between devices: 21.8 us -> 7.73 us  [shifted(): return lax.ppermute(value, 'mlp', [(i, (i + by) % 4) for i in range(4)])]
    ppermute x2 -> x1, waiting for transfers between devices: 13.8 us -> 0.01 us  [shards(): other = lax.ppermute(rows, 'core', [(0, 1), (1, 0)])]
    ppermute x9 -> x3, waiting for transfers between devices: 11.1 us -> 21.5 us  [shifted(): return lax.ppermute(value, 'mlp', [(i, (i + by) % 4) for i in range(4)])]
    slice x12 -> x5, local copies, waits for them, and re-layouts: 11.1 us -> 2.01 us  [the longest x1 0.8 us: shards(): weights = lax.all_gather(pieces[:, :PAD], ('x', 'y', 'core'))]
    squeeze x9 -> x0, local copies, waits for them, and re-layouts: 9.11 us -> none  [the longest x1 2.79 us: shards(): taken = lax.ppermute(slots[1], 'core', [(0, 1), (1, 0)])]
    all_to_all x6 -> x4, waiting for transfers between devices: 60.2 us -> 52 us  [swap(): return lax.all_to_all(value, axes, 0, 0, tiled=True)]
  transfers between devices with their start and end apart: 21 -> 10, of which waited for: 10 -> 4; matrix products, arithmetic and copies ran while one was open for 7% -> 2% of each run, Pallas kernels for 11% -> 12%
where the time goes in v3:
time: 408 us; the launch traced here: 407 us
  blocking collectives  158 us (39%)
  Pallas kernels  87.5 us (21%)
  waiting for transfers between devices  73.5 us (18%)
  starting transfers between devices  49.3 us (12%)
  local copies, waits for them, and re-layouts  21 us (5%)
  between operations  14.5 us (4%)
    all_to_all x6, blocking collectives, swap(): return lax.all_to_all(value, axes, 0, 0, tiled=True)  158 us
    all_to_all x4, waiting for transfers between devices, swap(): return lax.all_to_all(value, axes, 0, 0, tiled=True)  52 us
    all_to_all x4, starting transfers between devices, swap(): return lax.all_to_all(value, axes, 0, 0, tiled=True)  37 us
    ppermute x3, waiting for transfers between devices, shifted(): return lax.ppermute(value, 'mlp', [(i, (i + by) % 4) for i in range(4)])  21.5 us
    pallas_call x1, Pallas kernels, chain(): pl.pallas_call(chain_kernel, grid=(4,), in_specs=[whole((4, 3, LON, 768))...  17.8 us
    pallas_call x4, Pallas kernels, transform(): pl.pallas_call(table_kernel, grid=(3,), in_specs=[pl.BlockSpec((384, 1152...  17.3 us
    pallas_call x1, Pallas kernels, weight_grads(): pl.pallas_call(weight_grads_kernel, grid=(4, 2), in_specs=[whole((576, 76...  13.8 us
    unnamed x48, local copies, waits for them, and re-layouts  13.5 us
  transfers between devices with their start and end apart: 10, of which 4 were waited for; matrix products, arithmetic and copies ran while one was open for 2% of the time, Pallas kernels for 12%

profile of v3, /device:TPU:1, one launch (start us, length us, event | category | flops | bytes accessed | tf_op | source)
XLA Modules:
  0.0 406.8 jit_solution(8112358787978572699)
XLA Ops:
  12.5 10.0 %all-to-all-start = ((bf16[8,144,384]{2,1,0:T(8,128)(2,1)}), bf16[8,144,384]{2,1,0:T(8,128)(2,1)S(1)}, u32[]{:S(2)}, u32[]{:S(2)}) async-start(bf16[8,144,384]{2,1,0:T(8,128)(2,1)} %bitcast), calls=%async_computation | async-start | bytes 1769472 | tf_op jit(solution)/shard_map/all_to_all | solution.py:627
  22.8 3.6 collective-permute-start.2
  26.4 2.1 collective-permute-start.1
  28.4 2.1 collective-permute-start
  30.5 21.5 %collective-permute-done.2 = bf16[64,768]{1,0:T(8,128)(2,1)S(1)} collective-permute-done((bf16[64,768]{1,0:T(8,128)(2,1)S(1)}, bf16[64,768]{1,0:T(8,128)(2,1)S(1)}, u32[]{:S(2)}, u32[]{:S(2)}) %collective-permute-start.2) | collective-permute-done | bytes 98336 | tf_op jit(solution)/shard_map/ppermute | solution.py:631
  53.0 4.5 %shard_map.345 = bf16[1152,384]{1,0:T(8,128)(2,1)} custom-call(bf16[1152,1152]{1,0:T(8,128)(2,1)} %constant.92.clone.table, bf16[1152,384]{1,0:T(8,128)(2,1)S(1)} %bitcast.49), custom_call_target="tpu_custom_call" | custom-call | tf_op jit(solution)/shard_map/pallas_call | solution.py:179
  57.6 6.8 %all-to-all-start.1 = ((bf16[16,72,384]{2,1,0:T(8,128)(2,1)}), bf16[16,72,384]{2,1,0:T(8,128)(2,1)S(1)}, u32[]{:S(2)}, u32[]{:S(2)}) async-start(bf16[16,72,384]{2,1,0:T(8,128)(2,1)} %bitcast.2), calls=%async_computation.1 | async-start | bytes 1769472 | tf_op jit(solution)/shard_map/all_to_all | solution.py:627
  67.1 13.2 %all-to-all-done.1 = bf16[16,72,384]{2,1,0:T(8,128)(2,1)S(1)} async-done(((bf16[16,72,384]{2,1,0:T(8,128)(2,1)}), bf16[16,72,384]{2,1,0:T(8,128)(2,1)S(1)}, u32[]{:S(2)}, u32[]{:S(2)}) %all-to-all-start.1) | async-done | bytes 884768 | tf_op jit(solution)/shard_map/all_to_all | solution.py:627
  80.3 9.3 %shard_map.347 = (bf16[1152,384]{1,0:T(8,128)(2,1)S(1)}, bf16[576,768]{1,0:T(8,128)(2,1)S(1)}, f32[576,768]{1,0:T(8,128)}, bf16[576,768]{1,0:T(8,128)(2,1)S(1)}, f32[576,768]{1,0:T(8,128)}) custom-call(bf16[1152,384]{1,0:T(8,128)(2,1)S(1)} %bitcast.45, bf16[2,576,1152]{2,1,0:T(8,128)(2,1)} %constant.96.clone.fwd.inv_t, ...), custom_call_target="tpu_custom_call" | custom-call | tf_op jit(solution)/shard_map/pallas_call | solution.py:218
  90.5 25.5 %all_to_all.50 = bf16[16,72,384]{2,1,0:T(8,128)(2,1)S(1)} all-to-all(bf16[16,72,384]{2,1,0:T(8,128)(2,1)S(1)} %bitcast.55), channel_id=1, replica_groups=mesh['dp'=2,'x'=4,'y'=4,'core'=2,'mlp'=4] {'x','y'}, dimensions={0} | all-to-all | bytes 1769472 | tf_op jit(solution)/shard_map/all_to_all | solution.py:627
  116.0 4.5 %shard_map.348 = bf16[1152,384]{1,0:T(8,128)(2,1)} custom-call(bf16[1152,1152]{1,0:T(8,128)(2,1)} %constant.93.clone.table, bf16[1152,384]{1,0:T(8,128)(2,1)S(1)} %bitcast.50), custom_call_target="tpu_custom_call" | custom-call | tf_op jit(solution)/shard_map/pallas_call | solution.py:179
  120.5 11.9 %all-to-all-start.3 = ((bf16[8,144,384]{2,1,0:T(8,128)(2,1)}), bf16[8,144,384]{2,1,0:T(8,128)(2,1)S(1)}, u32[]{:S(2)}, u32[]{:S(2)}) async-start(bf16[8,144,384]{2,1,0:T(8,128)(2,1)} %bitcast.6), calls=%async_computation.3 | async-start | bytes 1769472 | tf_op jit(solution)/shard_map/all_to_all | solution.py:627
  132.4 2.2 copy.66.cotangent
  135.4 16.1 %all-to-all-done.3 = bf16[8,144,384]{2,1,0:T(8,128)(2,1)S(1)} async-done(((bf16[8,144,384]{2,1,0:T(8,128)(2,1)}), bf16[8,144,384]{2,1,0:T(8,128)(2,1)S(1)}, u32[]{:S(2)}, u32[]{:S(2)}) %all-to-all-start.3) | async-done | bytes 884768 | tf_op jit(solution)/shard_map/all_to_all | solution.py:627
  152.4 17.8 %shard_map.349 = (f32[576,768]{1,0:T(8,128)}, bf16[576,768]{1,0:T(8,128)(2,1)S(1)}, bf16[576,768]{1,0:T(8,128)(2,1)S(1)}, bf16[4,576,768]{2,1,0:T(8,128)(2,1)}, ...) custom-call(bf16[4,3,45,768]{3,2,1,0:T(8,128)(2,1)S(1)} %copy.64.x, ...), custom_call_target="tpu_custom_call" | custom-call | tf_op jit(solution)/shard_map/pallas_call | solution.py:394
  170.2 13.8 %shard_map.356 = bf16[16,2,4,48,768]{4,3,2,1,0:T(8,128)(2,1)} custom-call(bf16[576,768]{1,0:T(8,128)(2,1)S(1)} %get-tuple-element.60.mixed, bf16[4,576,768]{2,1,0:T(8,128)(2,1)} %get-tuple-element.61.grad_pre, bf16[4,576,768]{2,1,0:T(8,128)(2,1)} %get-tuple-element.48.hidden, bf16[576,768]{1,0:T(8,128)(2,1)S(1)} %get-tuple-element.62.grad_low), custom_call_target="tpu_custom_call" | custom-call | tf_op jit(solution)/shard_map/pallas_call | solution.py:454
  184.1 31.7 %all_to_all.51 = bf16[8,144,384]{2,1,0:T(8,128)(2,1)S(1)} all-to-all(bf16[8,144,384]{2,1,0:T(8,128)(2,1)S(1)} %bitcast.54), channel_id=1, replica_groups=mesh['dp'=2,'x'=4,'y'=4,'core'=2,'mlp'=4] {'core','mlp'}, dimensions={0} | all-to-all | bytes 1769472 | tf_op jit(solution)/shard_map/all_to_all | solution.py:627
  215.8 3.8 shard_map.351
  219.6 18.2 %all_to_all.52 = bf16[16,72,384]{2,1,0:T(8,128)(2,1)S(1)} all-to-all(bf16[16,72,384]{2,1,0:T(8,128)(2,1)S(1)} %bitcast.52), channel_id=1, replica_groups=mesh['dp'=2,'x'=4,'y'=4,'core'=2,'mlp'=4] {'x','y'}, dimensions={0} | all-to-all | bytes 1769472 | tf_op jit(solution)/shard_map/all_to_all | solution.py:627
  237.8 9.1 %shard_map.352 = (bf16[1152,384]{1,0:T(8,128)(2,1)S(1)}, bf16[576,768]{1,0:T(8,128)(2,1)S(1)}, bf16[576,768]{1,0:T(8,128)(2,1)S(1)}, f32[2,768]{1,0:T(2,128)S(1)}) custom-call(bf16[1152,384]{1,0:T(8,128)(2,1)S(1)} %bitcast.46, bf16[2,576,1152]{2,1,0:T(8,128)(2,1)} %constant.96.clone.fwd.inv_t, bf16[2,1152,576]{2,1,0:T(8,128)(2,1)} %constant.97.clone.inv.fwd_t, ...), custom_call_target="tpu_custom_call" | custom-call | tf_op jit(solution)/shard_map/pallas_call | solution.py:280
  246.9 3.2 shard_map.353
  250.3 26.5 %all_to_all.53 = bf16[16,88,384]{2,1,0:T(8,128)(2,1)S(1)} all-to-all(bf16[16,88,384]{2,1,0:T(8,128)(2,1)S(1)} %pad_maximum_fusion), channel_id=1, replica_groups=mesh['dp'=2,'x'=4,'y'=4,'core'=2,'mlp'=4] {'x','y'}, dimensions={0} | all-to-all | bytes 2162688 | tf_op jit(solution)/shard_map/all_to_all | solution.py:627
  276.9 4.5 %shard_map.354 = bf16[1152,384]{1,0:T(8,128)(2,1)} custom-call(bf16[1152,1152]{1,0:T(8,128)(2,1)} %constant.94.clone.table, bf16[1152,384]{1,0:T(8,128)(2,1)S(1)} %bitcast.53), custom_call_target="tpu_custom_call" | custom-call | tf_op jit(solution)/shard_map/pallas_call | solution.py:179
  281.3 8.4 %all-to-all-start.7 = ((bf16[8,144,384]{2,1,0:T(8,128)(2,1)}), bf16[8,144,384]{2,1,0:T(8,128)(2,1)S(1)}, u32[]{:S(2)}, u32[]{:S(2)}) async-start(bf16[8,144,384]{2,1,0:T(8,128)(2,1)} %bitcast.20), calls=%async_computation.7 | async-start | bytes 1769472 | tf_op jit(solution)/shard_map/all_to_all | solution.py:627
  290.7 22.6 %all-to-all-done.7 = bf16[8,144,384]{2,1,0:T(8,128)(2,1)S(1)} async-done(((bf16[8,144,384]{2,1,0:T(8,128)(2,1)}), bf16[8,144,384]{2,1,0:T(8,128)(2,1)S(1)}, u32[]{:S(2)}, u32[]{:S(2)}) %all-to-all-start.7) | async-done | bytes 884768 | tf_op jit(solution)/shard_map/all_to_all | solution.py:627
  313.3 2.9 shard_map.355
  319.4 25.9 %all_to_all.54 = bf16[8,72,768]{2,1,0:T(8,128)(2,1)S(1)} all-to-all(bf16[8,72,768]{2,1,0:T(8,128)(2,1)S(1)} %bitcast.62), channel_id=1, replica_groups=mesh['dp'=2,'x'=4,'y'=4,'core'=2,'mlp'=4] {'dp','mlp'}, dimensions={0} | all-to-all | bytes 1769472 | tf_op jit(solution)/shard_map/all_to_all | solution.py:627
  345.6 30.3 %all_to_all.55.own = bf16[16,96,768]{2,1,0:T(8,128)(2,1)S(1)} all-to-all(bf16[16,96,768]{2,1,0:T(8,128)(2,1)S(1)} %shard_map.357), channel_id=1, replica_groups=mesh['dp'=2,'x'=4,'y'=4,'core'=2,'mlp'=4] {'x','y'}, dimensions={0} | all-to-all | bytes 4718592 | tf_op jit(solution)/shard_map/all_to_all | solution.py:627
  375.9 4.6 %collective-permute-start.3 = (bf16[16,96,768]{2,1,0:T(8,128)(2,1)S(1)}, bf16[16,96,768]{2,1,0:T(8,128)(2,1)S(1)}, u32[]{:S(2)}, u32[]{:S(2)}) collective-permute-start(bf16[16,96,768]{2,1,0:T(8,128)(2,1)S(1)} %all_to_all.55.own), channel_id=1, source_target_pairs={{0,4},{4,0},{1,5},{5,1},{2,6},{6,2},{3,7},{7,3},{8,12},{12,8},{9,1... | collective-permute-start | bytes 7077896 | tf_op jit(solution)/shard_map/ppermute | solution.py:761
  380.6 6.7 %shard_map.350 = bf16[4,3,45,768]{3,2,1,0:T(8,128)(2,1)S(1)} custom-call(bf16[4,576,768]{2,1,0:T(8,128)(2,1)} %get-tuple-element.48.hidden, bf16[32,4,48,768]{3,2,1,0:T(8,128)(2,1)} %bitcast.60, f32[576,768]{1,0:T(8,128)S(1)} %copy-done.2, f32[576,1]{1,0:T(8,128)S(1)} %reshape.248.present, f32[1,768]{1,0:T(1,128)S(1)} %reshape.212.bias), custom_call_target="tpu_custom_call" | custom-call | tf_op jit(solution)/shard_map/pallas_call | solution.py:486
  388.6 2.2 copy.73
  392.3 5.2 %shard_map.358 = (f32[768,768]{1,0:T(8,128)}, f32[768,768]{1,0:T(8,128)}, f32[2,8,96,96]{3,2,1,0:T(8,128)}, f32[2,8,96,96]{3,2,1,0:T(8,128)}, f32[8,192]{1,0:T(8...) custom-call(s32[2]{0:T(128)S(1)} %pad_add_fusion.place, bf16[16,96,768]{2,1,0:T(8,128)(2,1)S(1)} %all_to_all.55.own, ...), custom_call_target="tpu_custom_call" | custom-call | tf_op jit(solution)/shard_map/pallas_call | solution.py:609
  (114 shorter events, 21.7 us)
Async XLA Ops:
  8.4 14.0 %copy-start.18 = (f32[768]{0:T(1024)S(1)}, f32[768]{0:T(1024)}, u32[]{:S(2)}) copy-start(f32[768]{0:T(1024)} %param.36) | copy-start | bytes 9220
  8.4 14.1 %copy-start.14 = (bf16[768,768]{1,0:T(8,128)(2,1)S(1)}, bf16[768,768]{1,0:T(8,128)(2,1)}, u32[]{:S(2)}) copy-start(bf16[768,768]{1,0:T(8,128)(2,1)} %param.35) | copy-start | bytes 3538948
  12.5 39.6 %all-to-all-start = ((bf16[8,144,384]{2,1,0:T(8,128)(2,1)}), bf16[8,144,384]{2,1,0:T(8,128)(2,1)S(1)}, u32[]{:S(2)}, u32[]{:S(2)}) async-start(bf16[8,144,384]{2,1,0:T(8,128)(2,1)} %bitcast), calls=%async_computation | async-start | bytes 1769472 | tf_op jit(solution)/shard_map/all_to_all | solution.py:627
  22.5 129.1 %all-gather.3.cloned.1.call-start = ((), (), s32[]{:S(2)}) async-start(), calls=%async_computation.12 | async-start | bytes 9732096 | tf_op jit(solution)/shard_map/all_gather | solution.py:691
  22.8 29.3 %collective-permute-start.2 = (bf16[64,768]{1,0:T(8,128)(2,1)S(1)}, bf16[64,768]{1,0:T(8,128)(2,1)S(1)}, u32[]{:S(2)}, u32[]{:S(2)}) collective-permute-start(bf16[64,768]{1,0:T(8,128)(2,1)S(1)} %concatenate.23), channel_id=1, source_target_pairs={{0,3},{1,0},{2,1},{3,2},{4,7},{5,4},{6,5},{7,6},{8,11},{9,8},{10,9... | collective-permute-start | bytes 294920 | tf_op jit(solution)/shard_map/ppermute | solution.py:631
  26.4 25.7 %collective-permute-start.1 = (bf16[64,768]{1,0:T(8,128)(2,1)S(1)}, bf16[64,768]{1,0:T(8,128)(2,1)S(1)}, u32[]{:S(2)}, u32[]{:S(2)}) collective-permute-start(bf16[64,768]{1,0:T(8,128)(2,1)S(1)} %concatenate.23), channel_id=1, source_target_pairs={{0,2},{1,3},{2,0},{3,1},{4,6},{5,7},{6,4},{7,5},{8,10},{9,11},{10,... | collective-permute-start | bytes 294920 | tf_op jit(solution)/shard_map/ppermute | solution.py:631
  28.4 23.6 %collective-permute-start = (bf16[64,768]{1,0:T(8,128)(2,1)S(1)}, bf16[64,768]{1,0:T(8,128)(2,1)S(1)}, u32[]{:S(2)}, u32[]{:S(2)}) collective-permute-start(bf16[64,768]{1,0:T(8,128)(2,1)S(1)} %concatenate.23), channel_id=1, source_target_pairs={{0,1},{1,2},{2,3},{3,0},{4,5},{5,6},{6,7},{7,4},{8,9},{9,10},{10,1... | collective-permute-start | bytes 294920 | tf_op jit(solution)/shard_map/ppermute | solution.py:631
  52.1 0.9 copy-start.13
  53.0 11.3 %copy-start.19 = (f32[2,2,96]{2,1,0:T(2,128)S(1)}, f32[2,2,96]{2,1,0:T(2,128)}, u32[]{:S(2)}) copy-start(f32[2,2,96]{2,1,0:T(2,128)} %param.30) | copy-start | bytes 4612
  53.0 11.5 %copy-start.20 = (f32[2,2,96]{2,1,0:T(2,128)S(1)}, f32[2,2,96]{2,1,0:T(2,128)}, u32[]{:S(2)}) copy-start(f32[2,2,96]{2,1,0:T(2,128)} %param.32) | copy-start | bytes 4612
  53.0 11.7 %copy-start.5 = (bf16[384,384]{1,0:T(8,128)(2,1)S(1)}, bf16[384,384]{1,0:T(8,128)(2,1)}, u32[]{:S(2)}) copy-start(bf16[384,384]{1,0:T(8,128)(2,1)} %constant.98.clone.mask) | copy-start | bytes 884740
  53.0 11.7 %copy-start.8 = (bf16[2,2,96,96]{3,2,1,0:T(8,128)(2,1)S(1)}, bf16[2,2,96,96]{3,2,1,0:T(8,128)(2,1)}, u32[]{:S(2)}) copy-start(bf16[2,2,96,96]{3,2,1,0:T(8,128)(2,1)} %w_in.1) | copy-start | bytes 221188
  53.0 11.7 %copy-start.9 = (bf16[2,2,96,96]{3,2,1,0:T(8,128)(2,1)S(1)}, bf16[2,2,96,96]{3,2,1,0:T(8,128)(2,1)}, u32[]{:S(2)}) copy-start(bf16[2,2,96,96]{3,2,1,0:T(8,128)(2,1)} %w_out.1) | copy-start | bytes 221188
  57.6 22.8 %all-to-all-start.1 = ((bf16[16,72,384]{2,1,0:T(8,128)(2,1)}), bf16[16,72,384]{2,1,0:T(8,128)(2,1)S(1)}, u32[]{:S(2)}, u32[]{:S(2)}) async-start(bf16[16,72,384]{2,1,0:T(8,128)(2,1)} %bitcast.2), calls=%async_computation.1 | async-start | bytes 1769472 | tf_op jit(solution)/shard_map/all_to_all | solution.py:627
  65.1 1.0 copy-start
  66.1 1.0 copy-start.1
  89.6 0.9 copy-start.6
  120.5 14.1 %copy-start.15 = (f32[768]{0:T(1024)S(1)}, f32[768]{0:T(1024)}, u32[]{:S(2)}) copy-start(f32[768]{0:T(1024)} %param.33) | copy-start | bytes 9220
  120.5 14.1 %copy-start.16 = (f32[768]{0:T(1024)S(1)}, f32[768]{0:T(1024)}, u32[]{:S(2)}) copy-start(f32[768]{0:T(1024)} %param.34) | copy-start | bytes 9220
  120.5 31.0 %all-to-all-start.3 = ((bf16[8,144,384]{2,1,0:T(8,128)(2,1)}), bf16[8,144,384]{2,1,0:T(8,128)(2,1)S(1)}, u32[]{:S(2)}, u32[]{:S(2)}) async-start(bf16[8,144,384]{2,1,0:T(8,128)(2,1)} %bitcast.6), calls=%async_computation.3 | async-start | bytes 1769472 | tf_op jit(solution)/shard_map/all_to_all | solution.py:627
  132.4 185.2 %reduce-scatter.2.cloned.1.call-start = ((), (), s32[]{:S(2)}) async-start(), calls=%async_computation.11 | async-start | bytes 9732096 | tf_op jit(solution)/shard_map/reduce_scatter | solution.py:727
  151.5 0.9 copy-start.11
  237.8 9.1 %copy-start.7 = (bf16[576,768]{1,0:T(8,128)(2,1)S(1)}, bf16[576,768]{1,0:T(8,128)(2,1)}, u32[]{:S(2)}) copy-start(bf16[576,768]{1,0:T(8,128)(2,1)} %copy-done.6) | copy-start | bytes 2654212
  237.8 9.2 %copy-start.10 = (bf16[384,128]{1,0:T(8,128)(2,1)S(1)}, bf16[384,128]{1,0:T(8,128)(2,1)}, u32[]{:S(2)}) copy-start(bf16[384,128]{1,0:T(8,128)(2,1)} %constant.99.clone.fold) | copy-start | bytes 294916
  281.3 32.0 %all-to-all-start.7 = ((bf16[8,144,384]{2,1,0:T(8,128)(2,1)}), bf16[8,144,384]{2,1,0:T(8,128)(2,1)S(1)}, u32[]{:S(2)}, u32[]{:S(2)}) async-start(bf16[8,144,384]{2,1,0:T(8,128)(2,1)} %bitcast.20), calls=%async_computation.7 | async-start | bytes 1769472 | tf_op jit(solution)/shard_map/all_to_all | solution.py:627
  316.2 1.2 copy-start.3
  345.6 34.9 %copy-start.17 = (f32[768]{0:T(1024)S(1)}, f32[768]{0:T(1024)}, u32[]{:S(2)}) copy-start(f32[768]{0:T(1024)} %param.38) | copy-start | bytes 9220
  345.6 35.0 %copy-start.2 = (f32[576,768]{1,0:T(8,128)S(1)}, f32[576,768]{1,0:T(8,128)}, u32[]{:S(2)}) copy-start(f32[576,768]{1,0:T(8,128)} %get-tuple-element.49.stream) | copy-start | bytes 5308420
  375.9 15.0 %collective-permute-start.3 = (bf16[16,96,768]{2,1,0:T(8,128)(2,1)S(1)}, bf16[16,96,768]{2,1,0:T(8,128)(2,1)S(1)}, u32[]{:S(2)}, u32[]{:S(2)}) collective-permute-start(bf16[16,96,768]{2,1,0:T(8,128)(2,1)S(1)} %all_to_all.55.own), channel_id=1, source_target_pairs={{0,4},{4,0},{1,5},{5,1},{2,6},{6,2},{3,7},{7,3},{8,12},{12,8},{9,1... | collective-permute-start | bytes 7077896 | tf_op jit(solution)/shard_map/ppermute | solution.py:761
  380.6 8.0 %copy-start.4 = (f32[4,3,45,768]{3,2,1,0:T(8,128)S(1)}, f32[4,3,45,768]{3,2,1,0:T(8,128)}, u32[]{:S(2)}) copy-start(f32[4,3,45,768]{3,2,1,0:T(8,128)} %copy-done.3) | copy-start | bytes 4976644
  390.9 1.4 copy-start.12
Sparse Core Ops, SparseCore 0:
  53.1 75.0 all-gather.2
  184.2 113.8 reduce-scatter.1
